TPU v7x, 256 devices: a whole 4x4x8 slice. The times are simulated.
256 devices in a mesh: grp: 64 (over z, x, core), rep: 4 (over y).
Axes of the slice: x: 4, y: 4, z: 8, core: 2. Of those that a mesh axis runs over, the one named last changes fastest.
Arguments:
- strain: bfloat16 [10240, 384], P(None, 'grp'), may hold values from -27 to 27
- fir_taps: float32 [64], replicated, may hold values from -0.75 to 0.75
- half_widths: int32 [10240], P('grp'), may hold values from 32 to 160
- pairs: int32 [256, 8], replicated, may hold values from -1 to 255, as said below
Outputs:
- correlations: bfloat16 [256, 8, 40, 40, 256], P(('grp', 'rep'))
Inputs may be any that keep to these rules, and one draw needn't show every extreme that they name: `pairs`: row e lists tile numbers; -1 marks an unused entry and used entries come first; no two used entries of a row lie in the same group of 4 consecutive tiles, none equals e; every row has a used entry and some row uses all 8.
All inputs are finite; a program needn't handle non-finite values.
Results may differ from a plain program's by a relative error of at most 0.0052.
Values may be sent and summed in bfloat16 or wider, within the bound.
A program may use at most 128 MiB of HBM per device.

v0:
```python
import math

import jax
import jax.numpy as jnp
from jax import lax
from jax.sharding import PartitionSpec as P

TILE = 40
LAGS = 256


def band_filter(samples, fir_taps):
    channels, length = samples.shape
    blocks = length // 128
    count = fir_taps.shape[0]
    rows_at = jnp.arange(128, dtype=jnp.int32)[:, None]
    cols_at = jnp.arange(128, dtype=jnp.int32)[None, :]
    tap_ids = jnp.arange(count, dtype=jnp.int32)
    near_gap = cols_at - rows_at
    far_gap = near_gap + 128
    taps_near = jnp.sum(
        jnp.where(near_gap[:, :, None] == tap_ids, fir_taps, jnp.float32(0.0)), axis=2
    )
    taps_far = jnp.sum(
        jnp.where(far_gap[:, :, None] == tap_ids, fir_taps, jnp.float32(0.0)), axis=2
    )
    blocked = samples.reshape(channels, blocks, 128)
    previous = jnp.concatenate(
        [jnp.zeros((channels, 1, 128), jnp.float32), blocked[:, :-1]], axis=1
    )
    result = jnp.einsum("cbs,st->cbt", blocked, taps_near, precision=lax.Precision.HIGHEST)
    result = result + jnp.einsum("cbs,st->cbt", previous, taps_far, precision=lax.Precision.HIGHEST)
    return result.reshape(channels, length)


def normalize(filtered, widths):
    channels, length = filtered.shape
    running = jnp.cumsum(jnp.abs(filtered), axis=1)
    prefix = jnp.concatenate([jnp.zeros((channels, 1), jnp.float32), running], axis=1)
    steps = jnp.arange(length, dtype=jnp.int32)[None, :]
    upper_end = jnp.minimum(steps + widths[:, None], length - 1) + 1
    lower_end = jnp.maximum(steps - widths[:, None], 0)
    window_sum = jnp.take_along_axis(prefix, upper_end, axis=1) - jnp.take_along_axis(
        prefix, lower_end, axis=1
    )
    level = window_sum / (2.0 * widths[:, None].astype(jnp.float32) + 1.0)
    return (filtered / (level + 1e-05)).astype(jnp.bfloat16)


def condition(samples, fir_taps, widths):
    return normalize(band_filter(samples.astype(jnp.float32), fir_taps), widths)


def lag_matrix(own, first, count, summed):
    tile_width, length = own.shape
    padded = jnp.concatenate(
        [
            jnp.zeros((tile_width, LAGS), own.dtype),
            own[:, :summed],
            jnp.zeros((tile_width, length - summed), own.dtype),
        ],
        axis=1,
    )
    shifted_rows = []
    for offset in range(count):
        begin = LAGS - (first + offset)
        shifted_rows.append(padded[:, begin : begin + length])
    return jnp.stack(shifted_rows, axis=1)


def correlate(own, chosen):
    listed, tile_width, length = chosen.shape
    summed = length - LAGS
    normalizer = 1.0 / math.sqrt(summed)
    lag_width = LAGS // 8
    flat = chosen.reshape(listed * tile_width, length)
    pieces = []
    for block_index in range(8):
        shifted = lag_matrix(own, block_index * lag_width, lag_width, summed)
        product = lax.dot_general(
            flat,
            shifted.reshape(tile_width * lag_width, length),
            (((1,), (1,)), ((), ())),
            preferred_element_type=jnp.float32,
        )
        pieces.append((product * normalizer).reshape(listed, tile_width, tile_width, lag_width))
    return jnp.concatenate(pieces, axis=3).astype(jnp.bfloat16)


def on_device(strain, fir_taps, half_widths, pairs):
    rep_count = lax.axis_size("rep")
    rep_index = lax.axis_index("rep")
    grp_index = lax.axis_index("grp")
    row_raw = lax.all_to_all(strain, "grp", split_axis=0, concat_axis=1, tiled=True)
    tile_width = TILE
    length = row_raw.shape[1]
    own_raw = lax.dynamic_slice_in_dim(row_raw, rep_index * tile_width, tile_width, 0)
    own_widths = lax.dynamic_slice_in_dim(half_widths, rep_index * tile_width, tile_width, 0)
    own = condition(own_raw, fir_taps, own_widths)
    row_tiles = lax.all_gather(own[None], "rep", axis=0, tiled=True)
    listed = pairs.shape[1]
    chosen_ids = lax.dynamic_index_in_dim(
        pairs, grp_index * rep_count + rep_index, 0, keepdims=False
    )
    empty = jnp.zeros((listed, tile_width, length), jnp.bfloat16)
    piece = lax.all_gather(row_tiles, "grp", axis=0, tiled=True)
    inside = (chosen_ids >= 0) & (chosen_ids < piece.shape[0])
    taken = jnp.take(piece, jnp.clip(chosen_ids, 0, piece.shape[0] - 1), axis=0)
    chosen = jnp.where(inside[:, None, None], taken, empty)
    return correlate(own, chosen)[None]


def solution(mesh):
    placed = (P(None, "grp"), P(), P("grp"), P())
    return jax.shard_map(
        on_device,
        mesh=mesh,
        in_specs=placed,
        out_specs=P(("grp", "rep"), None, None, None, None),
        check_vma=False,
    )
```

profile of v0, /device:TPU:1, one launch (start us, length us, event | category | flops | bytes accessed | tf_op | source)
XLA Modules:
  0.0 458.0 jit_solution(3430514163268576146)
XLA Ops:
  6.5 1.2 all_to_all.14
  8.7 13.0 %all-to-all-start = ((bf16[64,2,480]{2,1,0:T(2,128)(2,1)}), bf16[64,2,480]{2,1,0:T(2,128)(2,1)S(1)}, u32[]{:S(2)}, u32[]{:S(2)}) async-start(bf16[64,2,480]{2,1,0:T(2,128)(2,1)} %reshape.686), calls=%async_computation | async-start | bytes 262144 | tf_op jit(solution)/shard_map/all_to_all | solution.py:94
  22.7 3.5 select_reduce_fusion
  26.3 6.6 %all-to-all-done = bf16[64,2,480]{2,1,0:T(2,128)(2,1)S(1)} async-done(((bf16[64,2,480]{2,1,0:T(2,128)(2,1)}), bf16[64,2,480]{2,1,0:T(2,128)(2,1)S(1)}, u32[]{:S(2)}, u32[]{:S(2)}) %all-to-all-start) | async-done | bytes 122912 | tf_op jit(solution)/shard_map/all_to_all | solution.py:94
  35.2 121.4 %gather_fusion.2 = f32[15360]{0:T(1024)S(1)} fusion(f32[40,385]{1,0:T(8,128)S(1)} %concatenate.50, s32[15360]{0:T(1024)S(1)} %reshape.668), kind=kCustom, calls=%fused_computation.1.clone | custom fusion | bytes 245760 | tf_op jit(solution)/shard_map/jit(take_along_axis)/gather | solution.py:43
  156.6 121.4 %gather_fusion.1 = f32[15360]{0:T(1024)S(1)} fusion(f32[40,385]{1,0:T(8,128)S(1)} %concatenate.50, s32[15360]{0:T(1024)S(1)} %reshape.663), kind=kCustom, calls=%fused_computation.clone | custom fusion | bytes 245760 | tf_op jit(solution)/shard_map/jit(take_along_axis)/gather | solution.py:43
  278.2 10.9 %all-gather = bf16[160,384]{1,0:T(8,128)(2,1)} all-gather(bf16[40,384]{1,0:T(8,128)(2,1)S(1)} %get-tuple-element.9), channel_id=2, replica_groups=mesh['grp'=64,'rep'=4] {'rep'}, dimensions={0}, use_global_device_ids=true | all-gather | bytes 153600 | tf_op jit(solution)/shard_map/all_gather | solution.py:100
  293.4 0.9 copy-done.2
  295.5 1.1 copy.64
  300.4 1.1 copy.78
  301.5 1.1 copy.76
  302.6 1.1 copy.74
  303.7 1.1 copy.72
  304.8 63.8 %all-gather.3.cloned.1.call-done = bf16[256,40,384]{2,1,0:T(8,128)(2,1)} async-done(((bf16[4,40,384]{2,1,0:T(8,128)(2,1)}), bf16[256,40,384]{2,1,0:T(8,128)(2,1)}) %all-gather.3.cloned.1.call-update) | async-done | bytes 7864336 | tf_op jit(solution)/shard_map/all_gather | solution.py:106
  368.6 3.8 gather_fusion
  372.5 1.5 fusion.3
  374.1 1.5 fusion.2
  375.6 1.6 fusion.1
  377.2 1.5 fusion
  378.7 3.7 reshape.674
  382.4 4.8 %reshape.675 = bf16[1,8,40,40,32]{4,3,2,1,0:T(8,128)(2,1)} reshape(bf16[320,1280]{1,0:T(8,128)(2,1)} %fusion.1) | data formatting | bytes 1638400 | tf_op jit(solution)/shard_map/concatenate | solution.py:87
  387.2 4.8 %reshape.676 = bf16[1,8,40,40,32]{4,3,2,1,0:T(8,128)(2,1)} reshape(bf16[320,1280]{1,0:T(8,128)(2,1)} %fusion.2) | data formatting | bytes 1638400 | tf_op jit(solution)/shard_map/concatenate | solution.py:87
  392.0 4.9 %reshape.677 = bf16[1,8,40,40,32]{4,3,2,1,0:T(8,128)(2,1)} reshape(bf16[320,1280]{1,0:T(8,128)(2,1)} %fusion.3) | data formatting | bytes 1638400 | tf_op jit(solution)/shard_map/concatenate | solution.py:87
  396.9 2.8 fusion.7
  399.7 2.7 fusion.6
  402.4 2.7 fusion.5
  405.1 1.5 fusion.4
  406.6 4.8 %reshape.678 = bf16[1,8,40,40,32]{4,3,2,1,0:T(8,128)(2,1)} reshape(bf16[320,1280]{1,0:T(8,128)(2,1)} %fusion.4) | data formatting | bytes 1638400 | tf_op jit(solution)/shard_map/concatenate | solution.py:87
  411.4 4.8 %reshape.679 = bf16[1,8,40,40,32]{4,3,2,1,0:T(8,128)(2,1)} reshape(bf16[320,1280]{1,0:T(8,128)(2,1)} %fusion.5) | data formatting | bytes 1638400 | tf_op jit(solution)/shard_map/concatenate | solution.py:87
  416.3 4.8 %reshape.680 = bf16[1,8,40,40,32]{4,3,2,1,0:T(8,128)(2,1)} reshape(bf16[320,1280]{1,0:T(8,128)(2,1)} %fusion.6) | data formatting | bytes 1638400 | tf_op jit(solution)/shard_map/concatenate | solution.py:87
  421.1 4.8 %reshape.681 = bf16[1,8,40,40,32]{4,3,2,1,0:T(8,128)(2,1)} reshape(bf16[320,1280]{1,0:T(8,128)(2,1)} %fusion.7) | data formatting | bytes 1638400 | tf_op jit(solution)/shard_map/concatenate | solution.py:87
  425.9 25.2 %concatenate.61 = bf16[1,8,40,40,256]{4,3,2,1,0:T(8,128)(2,1)} concatenate(bf16[1,8,40,40,32]{4,3,2,1,0:T(8,128)(2,1)S(1)} %reshape.674, bf16[1,8,40,40,32]{4,3,2,1,0:T(8,128)(2,1)} %reshape.675, bf16[1,8,40,40,32]{4,3,2,1,0:T(8,128)(2,1)} %reshape.676, bf16[1,8,40,40,32]{4,3,2,1,0:T(8,128)(2,1)} %reshape.677, bf16[1,8,40,40,32]{4,3,2,1,0:T(8,128)(2,1)} %reshape.678, ...), dimensions={4} | concatenate | bytes 13107200 | tf_op jit(solution)/shard_map/concatenate | solution.py:87
  (110 shorter events, 13.3 us)
Async XLA Ops:
  8.7 24.1 %all-to-all-start = ((bf16[64,2,480]{2,1,0:T(2,128)(2,1)}), bf16[64,2,480]{2,1,0:T(2,128)(2,1)S(1)}, u32[]{:S(2)}, u32[]{:S(2)}) async-start(bf16[64,2,480]{2,1,0:T(2,128)(2,1)} %reshape.686), calls=%async_computation | async-start | bytes 262144 | tf_op jit(solution)/shard_map/all_to_all | solution.py:94
  21.7 346.8 %all-gather.3.cloned.1.call-start = ((), (), s32[]{:S(2)}) async-start(), calls=%async_computation.1 | async-start | bytes 7987200 | tf_op jit(solution)/shard_map/all_gather | solution.py:106
  156.6 121.5 %copy-start.5 = (pred[384]{0:T(512)(128)(4,1)S(1)}, pred[384]{0:T(512)(128)(4,1)}, u32[]{:S(2)}) copy-start(pred[384]{0:T(512)(128)(4,1)} %constant.46.clone.1) | copy-start | bytes 1156
  156.6 132.6 %copy-start.4 = (s32[256,8]{0,1:T(8,128)S(1)}, s32[256,8]{0,1:T(8,128)}, u32[]{:S(2)}) copy-start(s32[256,8]{0,1:T(8,128)} %param.9) | copy-start | bytes 24580
  293.4 0.9 copy-start.2
  294.3 1.2 copy-start.3
  372.4 4.7 %copy-start = (bf16[40,32,384]{2,1,0:T(8,128)(2,1)S(1)}, bf16[40,32,384]{2,1,0:T(8,128)(2,1)}, u32[]{:S(2)}) copy-start(bf16[40,32,384]{2,1,0:T(8,128)(2,1)} %copy.64) | copy-start | bytes 2949124
  396.9 8.2 %copy-start.1 = (bf16[40,32,384]{2,1,0:T(8,128)(2,1)S(1)}, bf16[40,32,384]{2,1,0:T(8,128)(2,1)}, u32[]{:S(2)}) copy-start(bf16[40,32,384]{2,1,0:T(8,128)(2,1)} %copy.72) | copy-start | bytes 2949124
Sparse Core Ops, SparseCore 0:
  289.3 79.2 all-gather.2
where the time goes:
time: 460 us; the launch traced here: 458 us
  local copies, waits for them, and re-layouts  327 us (71%)
  waiting for transfers between devices  70.4 us (15%)
  matrix products  16.4 us (4%)
  between operations  14 us (3%)
  starting transfers between devices  13 us (3%)
  blocking collectives  10.9 us (2%)
  other arithmetic  6.09 us (1%)
    gather x3, local copies, waits for them, and re-layouts, normalize(): jnp.take_along_axis(prefix, lower_end, axis=1)  121 us
    gather x3, local copies, waits for them, and re-layouts, normalize(): jnp.take_along_axis(prefix, upper_end, axis=1)  121 us
    all_gather x1, waiting for transfers between devices, on_device(): piece = lax.all_gather(row_tiles, 'grp', axis=0, tiled=True)  63.8 us
    concatenate x9, local copies, waits for them, and re-layouts, correlate(): return jnp.concatenate(pieces, axis=3).astype(jnp.bfloat16)  62.8 us
    dot_general x8, matrix products, correlate(): lax.dot_general(flat, shifted.reshape(tile_width * lag_width, length), ((...  15.8 us
    all_to_all x1, starting transfers between devices, on_device(): lax.all_to_all(strain, 'grp', split_axis=0, concat_axis=1, tiled=True)  13 us
    all_gather x1, blocking collectives, on_device(): row_tiles = lax.all_gather(own[None], 'rep', axis=0, tiled=True)  10.9 us
    unnamed x77, local copies, waits for them, and re-layouts  10 us
  transfers between devices with their start and end apart: 2, of which 2 were waited for; matrix products, arithmetic and copies ran while one was open for 4% of the time, Pallas kernels for 0%

commit v1 on v0

v1 whole, which is shorter than its diff:
```python
import functools
import math

import jax
import jax.numpy as jnp
from jax import lax
from jax.experimental import pallas as pl
from jax.experimental.pallas import tpu as pltpu
from jax.sharding import PartitionSpec as P

TILE = 40
NT = 384
LAGS = 256
TAPS = 64
PMAX = 8
TILES = 256
SUMMED = NT - LAGS
ROWS = 24
F32 = jnp.float32
BF16 = jnp.bfloat16
NT_DIMS = (((1,), (1,)), ((), ()))


def iota(shape, dim):
    return lax.broadcasted_iota(jnp.int32, shape, dim)


def exchange_kernel(n_grp, n_rep, x_ref, pairs_ref, hw_ref, r_ref, send, send_sem, recv_sem, local_sem):
    me = lax.axis_index("grp")
    rep = lax.axis_index("rep")
    barrier = pltpu.get_barrier_semaphore()

    def greet(k, carry):
        pl.semaphore_signal(
            barrier, inc=1, device_id={"grp": lax.rem(me + k, n_grp)}, device_id_type=pl.DeviceIdType.MESH
        )
        return carry

    lax.fori_loop(1, n_grp, greet, 0)

    rows = n_grp * PMAX
    row = iota((rows, TILES), 0)
    lane = iota((rows, TILES), 1)
    own_hot = jnp.where(lane == (row // PMAX) * n_rep + rep, 1.0, 0.0).astype(BF16)
    listed = lax.dot_general(
        own_hot, pairs_ref[...].astype(F32).astype(BF16), NT_DIMS, preferred_element_type=F32
    )
    slot = iota((rows, PMAX), 0) % PMAX
    ids = jnp.sum(jnp.where(iota((rows, PMAX), 1) == slot, listed, 0.0), axis=1, keepdims=True)
    pair_hot = jnp.where(lane.astype(F32) == ids, 1.0, 0.0).astype(BF16)
    x = x_ref[...]
    partner = jnp.dot(pair_hot, x, preferred_element_type=F32)
    own = jnp.dot(own_hot, x, preferred_element_type=F32)
    sub = iota((rows, 128), 0) % PMAX
    widths = hw_ref[...].astype(F32)
    tail = jnp.where(sub == 0, own[:, :128], 0.0)
    tail = jnp.where(sub == 1, own[:, 128:], tail)
    tail = jnp.where(sub == 2, jnp.broadcast_to(widths[0:1], (rows, 128)), tail)
    tail = jnp.where(sub == 3, jnp.broadcast_to(widths[1:2], (rows, 128)), tail)
    message = jnp.concatenate(
        [
            partner[:, :128].reshape(n_grp, PMAX, 128),
            partner[:, 128:].reshape(n_grp, PMAX, 128),
            tail.reshape(n_grp, PMAX, 128),
        ],
        axis=1,
    )
    send[...] = message.astype(BF16)

    pl.semaphore_wait(barrier, n_grp - 1)

    def ship(k, carry):
        to = lax.rem(me + k, n_grp)
        pltpu.make_async_remote_copy(
            src_ref=send.at[to],
            dst_ref=r_ref.at[me],
            send_sem=send_sem,
            recv_sem=recv_sem,
            device_id={"grp": to},
            device_id_type=pl.DeviceIdType.MESH,
        ).start()
        return carry

    lax.fori_loop(1, n_grp, ship, 0)
    local = pltpu.make_async_copy(send.at[me], r_ref.at[me], local_sem)
    local.start()
    local.wait()
    others = pl.ds(0, n_grp - 1)
    pltpu.make_async_copy(send.at[others], send.at[others], send_sem).wait()
    pltpu.make_async_copy(r_ref.at[others], r_ref.at[others], recv_sem).wait()


def split3(value):
    high = value.astype(BF16)
    rest = value - high.astype(F32)
    mid = rest.astype(BF16)
    low = (rest - mid.astype(F32)).astype(BF16)
    return high, mid, low


def correlate_kernel(n_grp, n_rep, r_ref, pairs_ref, taps_ref, out_ref, rf, raw, ab, own_ref, sc):
    step = pl.program_id(0)
    chan = (PMAX + 1) * TILE
    samples = NT // n_grp

    @pl.when(step == 0)
    def _():
        me = lax.axis_index("grp") * n_rep + lax.axis_index("rep")
        rf[...] = r_ref[...].astype(F32).reshape(n_grp * ROWS, 128)
        mine = jnp.where(iota((PMAX, TILES), 1) == me, pairs_ref[...], 0)
        ids = jnp.sum(mine.astype(F32), axis=1, keepdims=True)
        ids = jnp.concatenate([ids, jnp.full((PMAX, 1), me, jnp.int32).astype(F32)], axis=0)

        stair = pltpu.roll(
            jnp.broadcast_to(taps_ref[...], (8, 512)), 0, 1, stride=samples, stride_axis=0
        )
        shifted = [
            pltpu.roll(stair, samples * 8 * block + tt, 1)[:, :NT]
            for tt in range(samples)
            for block in range(n_grp // 8)
        ]
        fir = split3(jnp.concatenate(shifted, axis=0))

        for slot in range(PMAX + 1):
            first, second = (slot, PMAX + slot) if slot < PMAX else (2 * PMAX, 2 * PMAX + 1)
            low = rf[pl.ds(first, n_grp, stride=ROWS), :]
            high = rf[pl.ds(second, n_grp, stride=ROWS), :]
            turned = jnp.concatenate([low.T, high.T], axis=0)
            parts = [turned[TILE * tt : TILE * (tt + 1)] for tt in range(samples)]
            raw[TILE * slot : TILE * (slot + 1), :] = jnp.concatenate(parts, axis=1)

        samples_all = raw[...].astype(BF16)
        filtered = jnp.dot(samples_all, fir[2], preferred_element_type=F32)
        filtered = filtered + jnp.dot(samples_all, fir[1], preferred_element_type=F32)
        filtered = filtered + jnp.dot(samples_all, fir[0], preferred_element_type=F32)
        upper = jnp.where(iota((NT, NT), 0) <= iota((NT, NT), 1), 1.0, 0.0).astype(BF16)
        sizes = split3(jnp.abs(filtered))
        prefix = jnp.dot(sizes[2], upper, preferred_element_type=F32)
        prefix = prefix + jnp.dot(sizes[1], upper, preferred_element_type=F32)
        prefix = prefix + jnp.dot(sizes[0], upper, preferred_element_type=F32)

        width_low = rf[pl.ds(2 * PMAX + 2, n_grp, stride=ROWS), :].T
        width_high = rf[pl.ds(2 * PMAX + 3, n_grp, stride=ROWS), :].T
        width_rows = jnp.concatenate([width_low, width_high], axis=0)
        width_rows = jnp.concatenate(
            [width_rows[TILE * k : TILE * (k + 1)] for k in range(n_rep)], axis=1
        ).astype(BF16)
        spot = iota((2 * PMAX, TILES), 1)
        tile_at = n_rep * (spot % n_grp) + spot // n_grp
        hot = jnp.where(tile_at.astype(F32) == ids, 1.0, 0.0).astype(BF16)
        widths = lax.dot_general(width_rows, hot, NT_DIMS, preferred_element_type=F32)

        lane = iota((TILE, 128), 1)
        for slot in range(PMAX + 1):
            rows = slice(TILE * slot, TILE * (slot + 1))
            width_f = jnp.broadcast_to(widths[:, slot : slot + 1], (TILE, 128))
            width = width_f.astype(jnp.int32)
            up = lane + width
            down = lane - width - 1
            up_at, up_block = up & 127, up >> 7
            down_at, down_block = down & 127, down >> 7
            blocks = [prefix[rows, 128 * b : 128 * (b + 1)] for b in range(3)]
            ups = [jnp.take_along_axis(block, up_at, axis=1) for block in blocks]
            downs = [jnp.take_along_axis(block, down_at, axis=1) for block in blocks]
            total = jnp.broadcast_to(blocks[2][:, 127:128], (TILE, 128))
            scale = 1.0 / (2.0 * width_f + 1.0)
            for b in range(3 if slot < PMAX else 1):
                later = [ups[k] if k < 3 else total for k in range(b, b + 3)]
                end = jnp.where(up_block == 0, later[0], jnp.where(up_block == 1, later[1], later[2]))
                begin = jnp.where(down_block == 0, downs[b], 0.0)
                if b >= 1:
                    begin = jnp.where(down_block == -1, downs[b - 1], begin)
                if b >= 2:
                    begin = jnp.where(down_block == -2, downs[b - 2], begin)
                level = (end - begin) * scale
                white = filtered[rows, 128 * b : 128 * (b + 1)] / (level + 1e-05)
                if slot < PMAX:
                    raw[rows, 128 * b : 128 * (b + 1)] = white
                else:
                    own_ref[...] = white.astype(BF16).astype(F32)
        count = PMAX * TILE
        whitened = raw[0:count, :].astype(BF16)
        ab[0:count, :] = whitened[:, 0:256]
        ab[count:, :] = whitened[:, 128:384]

    count = PMAX * TILE
    normalizer = 1.0 / math.sqrt(SUMMED)
    earlier = iota((128, 128), 1) < iota((128, 128), 0)

    def two_channels(pair, carry):
        weights = []
        for k in range(2):
            line = own_ref[pl.ds(16 * step + 2 * pair + k, 1), :]
            turned = pltpu.roll(jnp.broadcast_to(line, (128, 128)), 0, 1, stride=1, stride_axis=0)
            weights.append(
                jnp.concatenate([jnp.where(earlier, 0.0, turned), jnp.where(earlier, turned, 0.0)], axis=1)
            )
        weight = jnp.concatenate(weights, axis=0).astype(BF16)
        product = lax.dot_general(ab[...], weight, NT_DIMS, preferred_element_type=F32) * normalizer
        for k in range(2):
            for half in range(2):
                sc[half, pl.ds(2 * pair + k, count, stride=16), :] = product[
                    count * half : count * (half + 1), 128 * k : 128 * (k + 1)
                ]
        return carry

    lax.fori_loop(0, jnp.minimum(8, (TILE - 16 * step) // 2), two_channels, 0)
    for p in range(PMAX):
        for half in range(2):
            piece = sc[half, 16 * TILE * p : 16 * TILE * (p + 1), :]
            out_ref[0, p, :, :, 128 * half : 128 * (half + 1)] = piece.reshape(TILE, 16, 128).astype(BF16)


def on_device(n_grp, n_rep, strain, fir_taps, half_widths, pairs):
    samples = strain.shape[1]
    x = strain.reshape(TILES, TILE, samples).transpose(0, 2, 1).reshape(TILES, TILE * samples)
    x = jnp.pad(x, ((0, 0), (0, 256 - TILE * samples)))
    widths = jnp.pad(half_widths, (0, 256 - half_widths.shape[0])).reshape(2, 128)
    turned_pairs = pairs.T
    taps = jnp.pad(fir_taps, (0, 512 - TAPS)).reshape(1, 512)
    vmem = pl.BlockSpec(memory_space=pltpu.VMEM)
    received = pl.pallas_call(
        functools.partial(exchange_kernel, n_grp, n_rep),
        out_shape=jax.ShapeDtypeStruct((n_grp, ROWS, 128), BF16),
        in_specs=[vmem] * 3,
        out_specs=pl.BlockSpec(memory_space=pl.ANY),
        scratch_shapes=[
            pltpu.VMEM((n_grp, ROWS, 128), BF16),
            pltpu.SemaphoreType.DMA,
            pltpu.SemaphoreType.DMA,
            pltpu.SemaphoreType.DMA,
        ],
        compiler_params=pltpu.CompilerParams(
            collective_id=0, has_side_effects=True, vmem_limit_bytes=32 * 1024 * 1024
        ),
        name="exchange",
    )(x, turned_pairs, widths)
    chan = (PMAX + 1) * TILE
    whole = lambda *shape: pl.BlockSpec(shape, lambda i: (0,) * len(shape))
    return pl.pallas_call(
        functools.partial(correlate_kernel, n_grp, n_rep),
        out_shape=jax.ShapeDtypeStruct((1, PMAX, TILE, TILE, LAGS), BF16),
        grid=(3,),
        in_specs=[whole(n_grp, ROWS, 128), whole(PMAX, TILES), whole(1, 512)],
        out_specs=pl.BlockSpec((1, PMAX, TILE, 16, LAGS), lambda i: (0, 0, 0, i, 0)),
        scratch_shapes=[
            pltpu.VMEM((n_grp * ROWS, 128), F32),
            pltpu.VMEM((chan, NT), F32),
            pltpu.VMEM((2 * PMAX * TILE, 256), BF16),
            pltpu.VMEM((TILE, 128), F32),
            pltpu.VMEM((2, PMAX * TILE * 16, 128), F32),
        ],
        compiler_params=pltpu.CompilerParams(vmem_limit_bytes=48 * 1024 * 1024),
        name="correlate",
    )(received, turned_pairs, taps)


def solution(mesh):
    placed = (P(None, "grp"), P(), P("grp"), P())
    return jax.shard_map(
        functools.partial(on_device, mesh.shape["grp"], mesh.shape["rep"]),
        mesh=mesh,
        in_specs=placed,
        out_specs=P(("grp", "rep"), None, None, None, None),
        check_vma=False,
    )
```

time: 460 us -> 41.4 us (0.09)
  local copies, waits for them, and re-layouts: 327 us -> 4.58 us
  waiting for transfers between devices: 70.4 us -> 0 us
  Pallas kernels: 0 us -> 36.6 us
  matrix products: 16.4 us -> 0 us
  between operations: 14 us -> 0.06 us
  starting transfers between devices: 13 us -> 0 us
  blocking collectives: 10.9 us -> 0 us
  other arithmetic: 6.09 us -> 0 us
    gather x7 -> x0, local copies, waits for them, and re-layouts: 247 us -> none  [the longest x3 121 us: normalize(): jnp.take_along_axis(prefix, lower_end, axis=1)]
    all_gather x1 -> x0, waiting for transfers between devices: 63.8 us -> none  [on_device(): piece = lax.all_gather(row_tiles, 'grp', axis=0, tiled=True)]
    concatenate x10 -> x0, local copies, waits for them, and re-layouts: 62.9 us -> none  [the longest x9 62.8 us: correlate(): return jnp.concatenate(pieces, axis=3).astype(jnp.bfloat16)]
    pallas_call x0 -> x2, Pallas kernels: none -> 36.6 us  [the longest x1 21.7 us: on_device(): pl.pallas_call(functools.partial(exchange_kernel, n_grp, n_rep), out_shap...]
    dot_general x10 -> x0, matrix products: 16.4 us -> none  [the longest x8 15.8 us: correlate(): lax.dot_general(flat, shifted.reshape(tile_width * lag_width, length), ((...]
    all_to_all x1 -> x0, starting transfers between devices: 13 us -> none  [on_device(): lax.all_to_all(strain, 'grp', split_axis=0, concat_axis=1, tiled=True)]
    all_gather x1 -> x0, blocking collectives: 10.9 us -> none  [on_device(): row_tiles = lax.all_gather(own[None], 'rep', axis=0, tiled=True)]
    unnamed x77 -> x4, local copies, waits for them, and re-layouts: 10 us -> 1.38 us
  transfers between devices with their start and end apart: 2 -> 0, of which waited for: 2 -> 0; matrix products, arithmetic and copies ran while one was open for 4% -> 0% of each run, Pallas kernels for 0% -> 0%
where the time goes in v1:
time: 41.4 us; the launch traced here: 41.2 us
  Pallas kernels  36.6 us (88%)
  local copies, waits for them, and re-layouts  4.58 us (11%)
    pallas_call x1, Pallas kernels, on_device(): pl.pallas_call(functools.partial(exchange_kernel, n_grp, n_rep), out_shap...  21.7 us
    pallas_call x1, Pallas kernels, on_device(): pl.pallas_call(functools.partial(correlate_kernel, n_grp, n_rep), out_sha...  14.9 us
    reshape x2, local copies, waits for them, and re-layouts, on_device(): strain.reshape(TILES, TILE, samples).transpose(0, 2, 1)  1.68 us
    unnamed x4, local copies, waits for them, and re-layouts  1.38 us

profile of v1, /device:TPU:1, one launch (start us, length us, event | category | flops | bytes accessed | tf_op | source)
XLA Modules:
  0.0 41.2 jit_solution(7725475857230277476)
XLA Ops:
  0.0 0.7 %pad_bitcast_fusion.hw_ref = s32[2,128]{1,0:T(2,128)S(1)} fusion(s32[160]{0:T(256)} %param.6), kind=kLoop, calls=%fused_computation | loop fusion | bytes 1664 | tf_op jit(solution)/shard_map/reshape | solution.py:218
  0.7 0.7 %pad.14 = f32[512]{0:T(512)S(1)} pad(f32[64]{0:T(128)} %param.5, f32[]{:T(128)} %constant.5.clone.1), padding=0_448 | pad | bytes 2308 | tf_op jit(solution)/shard_map/jit(_pad)/pad | solution.py:220
  1.3 1.6 %reshape.12 = bf16[256,40,6]{1,0,2:T(8,128)(2,1)S(1)} reshape(bf16[10240,6]{0,1:T(8,128)(2,1)} %param.4) | data formatting | bytes 245760 | tf_op jit(solution)/shard_map/reshape | solution.py:216
  2.9 0.2 copy.6
  3.1 0.1 copy.7
  3.2 0.0 copy-start
  3.2 0.7 %copy-done = s32[256,8]{0,1:T(8,128)S(1)} copy-done((s32[256,8]{0,1:T(8,128)S(1)}, s32[256,8]{0,1:T(8,128)}, u32[]{:S(2)}) %copy-start) | copy-done | bytes 8216
  3.9 21.7 %exchange.1.r_ref = bf16[64,24,128]{2,1,0:T(8,128)(2,1)S(1)} custom-call(bf16[256,256]{1,0:T(8,128)(2,1)S(1)} %pad.12.x_ref, s32[8,256]{1,0:T(8,128)S(1)} %bitcast.8, s32[2,128]{1,0:T(2,128)S(1)} %pad_bitcast_fusion.hw_ref), custom_call_target="tpu_custom_call" | custom-call | tf_op jit(solution)/shard_map/exchange/pallas_call | solution.py:222
  25.6 0.0 copy-start.1
  25.6 0.7 %copy-done.1 = s32[256,8]{0,1:T(8,128)S(1)} copy-done((s32[256,8]{0,1:T(8,128)S(1)}, s32[256,8]{0,1:T(8,128)}, u32[]{:S(2)}) %copy-start.1) | copy-done | bytes 8216
  26.3 14.9 %correlate.1 = bf16[1,8,40,40,256]{4,3,2,1,0:T(8,128)(2,1)} custom-call(bf16[64,24,128]{2,1,0:T(8,128)(2,1)S(1)} %exchange.1.r_ref, s32[8,256]{1,0:T(8,128)S(1)} %bitcast.9, f32[1,512]{1,0:T(1,128)S(1)} %bitcast.10), custom_call_target="tpu_custom_call" | custom-call | tf_op jit(solution)/shard_map/correlate/pallas_call | solution.py:240
  (1 shorter events, 0.0 us)
Async XLA Ops:
  3.2 0.7 %copy-start = (s32[256,8]{0,1:T(8,128)S(1)}, s32[256,8]{0,1:T(8,128)}, u32[]{:S(2)}) copy-start(s32[256,8]{0,1:T(8,128)} %param.7) | copy-start | bytes 24580
  25.6 0.7 %copy-start.1 = (s32[256,8]{0,1:T(8,128)S(1)}, s32[256,8]{0,1:T(8,128)}, u32[]{:S(2)}) copy-start(s32[256,8]{0,1:T(8,128)} %param.7) | copy-start | bytes 24580

commit v2 on v0

v2 whole, which is shorter than its diff:
```python
import functools
import math

import jax
import jax.numpy as jnp
from jax import lax
from jax.experimental import pallas as pl
from jax.experimental.pallas import tpu as pltpu
from jax.sharding import PartitionSpec as P

TILE = 40
NT = 384
LAGS = 256
TAPS = 64
PMAX = 8
TILES = 256
SUMMED = NT - LAGS
HALF = PMAX // 2
LINES = HALF * TILE
BAND = 8
F32 = jnp.float32
BF16 = jnp.bfloat16
NT_DIMS = (((1,), (1,)), ((), ()))
MESH = pl.DeviceIdType.MESH


def iota(shape, dim):
    return lax.broadcasted_iota(jnp.int32, shape, dim)


def one_hot(where):
    return jnp.where(where, 1.0, 0.0).astype(BF16)


def split3(value):
    high = value.astype(BF16)
    rest = value - high.astype(F32)
    mid = rest.astype(BF16)
    low = (rest - mid.astype(F32)).astype(BF16)
    return high, mid, low


def wide_row(row):
    return jnp.concatenate([row, jnp.zeros((1, 128 - row.shape[1]), row.dtype)], axis=1)


def pack_messages(n_grp, n_rep, rep, samples, strain, pairs, widths, rows_f, sends):
    groups = TILES // 16
    span = 16 * TILE
    for g in range(groups):
        for k in range(span // 128):
            at = span * g + 128 * k
            rows_f[k, 8 * g : 8 * g + samples, :] = strain[:, at : at + 128].astype(F32)
    times = [
        jnp.concatenate([rows_f[k, pl.ds(t, groups, stride=8), :] for k in range(span // 128)], axis=1)
        for t in range(samples)
    ]
    blank = jnp.zeros((groups, 256 - TILE * samples), F32)
    x = jnp.concatenate(
        [
            jnp.concatenate([part[:, TILE * m : TILE * (m + 1)] for part in times] + [blank], axis=1)
            for m in range(16)
        ],
        axis=0,
    ).astype(BF16)

    rows = n_grp * 8
    row = iota((rows, TILES), 0)
    lane = iota((rows, TILES), 1)
    tile = 16 * (lane % 16) + lane // 16
    home = (row // 8) * n_rep + rep
    listed = lax.dot_general(
        one_hot(lane == home), pairs.astype(F32).astype(BF16), NT_DIMS, preferred_element_type=F32
    )
    sub = iota((rows, PMAX), 0) % 8
    slot = iota((rows, PMAX), 1)
    upper = iota((rows, 128), 0) % 8
    own = jnp.dot(one_hot(tile == home), x, preferred_element_type=F32)
    block = jnp.where(upper == 0, own[:, :128], 0.0)
    block = jnp.where(upper == 1, own[:, 128:], block)
    block = jnp.where(upper == 2, jnp.broadcast_to(widths[0], (rows, 128)), block)
    block = jnp.where(upper == 3, jnp.broadcast_to(widths[1], (rows, 128)), block)
    sends[0][...] = block.reshape(n_grp, 8, 128).astype(BF16)
    for part in range(2):
        ids = jnp.sum(
            jnp.where(slot == sub % HALF + HALF * part, listed, 0.0), axis=1, keepdims=True
        )
        taken = jnp.dot(one_hot(tile.astype(F32) == ids), x, preferred_element_type=F32)
        block = jnp.where(upper < HALF, taken[:, :128], taken[:, 128:])
        sends[1 + part][...] = block.reshape(n_grp, 8, 128).astype(BF16)


def fir_matrix(n_grp, samples, taps):
    stair = pltpu.roll(jnp.broadcast_to(wide_row(taps), (8, 128)), 0, 1, stride=samples, stride_axis=0)
    lane = iota((8, 128), 1)
    zero = jnp.zeros((8, 128), F32)
    strips = []
    for tt in range(samples):
        for block in range(n_grp // 8):
            shift = samples * 8 * block + tt
            first, by = shift // 128, shift % 128
            turned = pltpu.roll(stair, by, 1) if by else stair
            columns = [zero] * (NT // 128 + 1)
            columns[first] = jnp.where(lane >= by, turned, 0.0)
            columns[first + 1] = jnp.where(lane < by, turned, 0.0)
            strips.append(jnp.concatenate(columns[: NT // 128], axis=1))
    return split3(jnp.concatenate(strips, axis=0))


def unfold(n_grp, samples, flat, low_row, high_row):
    low = flat[pl.ds(low_row, n_grp, stride=8), :]
    high = flat[pl.ds(high_row, n_grp, stride=8), :]
    turned = jnp.concatenate([low.T, high.T], axis=0)
    parts = [turned[TILE * tt : TILE * (tt + 1)] for tt in range(samples)]
    return jnp.concatenate(parts, axis=1)


def filter_and_sum(raw, fir, upper):
    raw = raw.astype(BF16)
    filtered = jnp.dot(raw, fir[2], preferred_element_type=F32)
    filtered = filtered + jnp.dot(raw, fir[1], preferred_element_type=F32)
    filtered = filtered + jnp.dot(raw, fir[0], preferred_element_type=F32)
    sizes = split3(jnp.abs(filtered))
    prefix = jnp.dot(sizes[2], upper, preferred_element_type=F32)
    prefix = prefix + jnp.dot(sizes[1], upper, preferred_element_type=F32)
    prefix = prefix + jnp.dot(sizes[0], upper, preferred_element_type=F32)
    return filtered, prefix


def whiten(filtered, prefix, width_f, blocks_out):
    lane = iota((TILE, 128), 1)
    width_f = jnp.broadcast_to(width_f, (TILE, 128))
    width = width_f.astype(jnp.int32)
    up = lane + width
    down = lane - width - 1
    up_at, up_block = up & 127, up >> 7
    down_at, down_block = down & 127, down >> 7
    blocks = [prefix[:, 128 * b : 128 * (b + 1)] for b in range(3)]
    ups = [jnp.take_along_axis(block, up_at, axis=1) for block in blocks]
    downs = [jnp.take_along_axis(block, down_at, axis=1) for block in blocks]
    total = jnp.broadcast_to(blocks[2][:, 127:128], (TILE, 128))
    scale = 1.0 / (2.0 * width_f + 1.0)
    results = []
    for b in range(blocks_out):
        later = [ups[k] if k < 3 else total for k in range(b, b + 3)]
        end = jnp.where(up_block == 0, later[0], jnp.where(up_block == 1, later[1], later[2]))
        begin = jnp.where(down_block == 0, downs[b], 0.0)
        if b >= 1:
            begin = jnp.where(down_block == -1, downs[b - 1], begin)
        if b >= 2:
            begin = jnp.where(down_block == -2, downs[b - 2], begin)
        level = (end - begin) * scale
        results.append(filtered[:, 128 * b : 128 * (b + 1)] / (level + 1e-05))
    return results


def exchange_kernel(
    n_grp, n_rep, strain_hbm, pairs_hbm, widths_hbm, taps_hbm, w_ref, ab_ref,
    strain, pairs, widths, taps, rows_f, flat, own_ref,
    send_0, send_1, send_2, got_0, got_1, got_2, in_sems, send_sems, recv_sems, local_sems,
):
    me = lax.axis_index("grp")
    rep = lax.axis_index("rep")
    samples = NT // n_grp
    barrier = pltpu.get_barrier_semaphore()
    loads = [
        pltpu.make_async_copy(source, target, in_sems.at[k])
        for k, (source, target) in enumerate(
            [(strain_hbm, strain), (pairs_hbm, pairs), (widths_hbm, widths), (taps_hbm, taps)]
        )
    ]
    for load in loads:
        load.start()

    def greet(k, carry):
        pl.semaphore_signal(
            barrier, inc=1, device_id={"grp": lax.rem(me + k, n_grp)}, device_id_type=MESH
        )
        return carry

    lax.fori_loop(1, n_grp, greet, 0)
    for load in loads:
        load.wait()

    sends = (send_0, send_1, send_2)
    gots = (got_0, got_1, got_2)
    count = widths.shape[1]
    width_rows = [widths[:, 0:128].astype(F32), wide_row(widths[:, 128:count].astype(F32))]
    pack_messages(n_grp, n_rep, rep, samples, strain, pairs[...], width_rows, rows_f, sends)

    pl.semaphore_wait(barrier, n_grp - 1)
    for wave in range(3):

        def ship(k, carry):
            half = (k + 1) // 2
            to = lax.rem(me + jnp.where(k % 2 == 1, half, n_grp - half), n_grp)
            pltpu.make_async_remote_copy(
                src_ref=sends[wave].at[to],
                dst_ref=gots[wave].at[me],
                send_sem=send_sems.at[wave],
                recv_sem=recv_sems.at[wave],
                device_id={"grp": to},
                device_id_type=MESH,
            ).start()
            return carry

        lax.fori_loop(1, n_grp, ship, 0)
        pltpu.make_async_copy(sends[wave].at[me], gots[wave].at[me], local_sems.at[wave]).start()

    others = pl.ds(0, n_grp - 1)

    def arrive(wave):
        pltpu.make_async_copy(sends[wave].at[me], gots[wave].at[me], local_sems.at[wave]).wait()
        pltpu.make_async_copy(gots[wave].at[others], gots[wave].at[others], recv_sems.at[wave]).wait()
        flat[...] = gots[wave][...].astype(F32).reshape(n_grp * 8, 128)

    fir = fir_matrix(n_grp, samples, taps[...])
    upper = one_hot(iota((NT, NT), 0) <= iota((NT, NT), 1))
    tile = me * n_rep + rep
    mine = jnp.where(iota((PMAX, TILES), 1) == tile, pairs[...], 0)
    ids = jnp.sum(mine.astype(F32), axis=1, keepdims=True)
    ids = jnp.concatenate([ids, jnp.full((PMAX, 1), tile, jnp.int32).astype(F32)], axis=0)
    spot = iota((2 * PMAX, TILES), 1)
    hot = one_hot((n_rep * (spot % n_grp) + spot // n_grp).astype(F32) == ids)

    arrive(0)
    turned = jnp.concatenate(
        [flat[pl.ds(2, n_grp, stride=8), :].T, flat[pl.ds(3, n_grp, stride=8), :].T], axis=0
    )
    turned = jnp.concatenate([turned[TILE * k : TILE * (k + 1)] for k in range(n_rep)], axis=1)
    spans = lax.dot_general(turned.astype(BF16), hot, NT_DIMS, preferred_element_type=F32)
    filtered, prefix = filter_and_sum(unfold(n_grp, samples, flat, 0, 1), fir, upper)
    own = whiten(filtered, prefix, spans[:, PMAX : PMAX + 1], 1)[0].astype(BF16).astype(F32)
    own_ref[...] = jnp.take_along_axis(own, 127 - iota((TILE, 128), 1), axis=1)
    later = iota((128, 128), 1) > iota((128, 128), 0)

    def toeplitz(pair, carry):
        for k in range(2):
            line = own_ref[pl.ds(2 * pair + k, 1), :]
            turned = pltpu.roll(jnp.broadcast_to(line, (128, 128)), 1, 1, stride=1, stride_axis=0)
            w_ref[pair, 0:128, 128 * k : 128 * (k + 1)] = jnp.where(later, 0.0, turned).astype(BF16)
            w_ref[pair, 128:256, 128 * k : 128 * (k + 1)] = jnp.where(later, turned, 0.0).astype(BF16)
        return carry

    lax.fori_loop(0, TILE // 2, toeplitz, 0)

    for part in range(2):
        arrive(1 + part)
        raw = jnp.concatenate(
            [unfold(n_grp, samples, flat, slot, HALF + slot) for slot in range(HALF)], axis=0
        )
        filtered, prefix = filter_and_sum(raw, fir, upper)
        columns = [[], [], []]
        for slot in range(HALF):
            rows = slice(TILE * slot, TILE * (slot + 1))
            at = HALF * part + slot
            white = whiten(filtered[rows], prefix[rows], spans[:, at : at + 1], 3)
            for b in range(3):
                columns[b].append(white[b])
        white = [jnp.concatenate(column, axis=0).astype(BF16) for column in columns]
        ab_ref[part, 0:LINES, 0:128] = white[0]
        ab_ref[part, 0:LINES, 128:256] = white[1]
        ab_ref[part, LINES : 2 * LINES, 0:128] = white[1]
        ab_ref[part, LINES : 2 * LINES, 128:256] = white[2]

    for wave in range(3):
        pltpu.make_async_copy(sends[wave].at[others], sends[wave].at[others], send_sems.at[wave]).wait()


def correlate_kernel(w_ref, ab_ref, out_ref, sc_a, sc_b, done, sems):
    normalizer = 1.0 / math.sqrt(SUMMED)
    copies = []
    turn = 0
    for part in range(2):
        for at in range(0, TILE, BAND):
            sc = (sc_a, sc_b)[turn % 2]
            turn += 1
            for pair in range(BAND // 2):
                product = jnp.dot(ab_ref[part], w_ref[at // 2 + pair], preferred_element_type=F32)
                product = product * normalizer
                for k in range(2):
                    for half in range(2):
                        sc[half, pl.ds(2 * pair + k, LINES, stride=BAND), :] = product[
                            LINES * half : LINES * (half + 1), 128 * k : 128 * (k + 1)
                        ]
            piece = jnp.concatenate([sc[0], sc[1]], axis=1)
            done[part, :, :, at : at + BAND, :] = piece.reshape(HALF, TILE, BAND, LAGS).astype(BF16)
        copy = pltpu.make_async_copy(done.at[part], out_ref.at[0, pl.ds(HALF * part, HALF)], sems.at[part])
        copy.start()
        copies.append(copy)
    for copy in copies:
        copy.wait()


def on_device(n_grp, n_rep, strain, fir_taps, half_widths, pairs):
    vmem = pl.BlockSpec(memory_space=pltpu.VMEM)
    hbm = pl.BlockSpec(memory_space=pltpu.HBM)
    samples, channels = strain.shape[1], strain.shape[0]
    block = pltpu.VMEM((n_grp, 8, 128), BF16)
    weights, lines = pl.pallas_call(
        functools.partial(exchange_kernel, n_grp, n_rep),
        out_shape=(
            jax.ShapeDtypeStruct((TILE // 2, 256, 256), BF16),
            jax.ShapeDtypeStruct((2, 2 * LINES, 256), BF16),
        ),
        in_specs=[hbm] * 4,
        out_specs=(vmem, vmem),
        scratch_shapes=[
            pltpu.VMEM((samples, channels), BF16),
            pltpu.VMEM((PMAX, TILES), jnp.int32),
            pltpu.VMEM((1, half_widths.shape[0]), jnp.int32),
            pltpu.VMEM((1, TAPS), F32),
            pltpu.VMEM((16 * TILE // 128, 8 * TILES // 16, 128), F32),
            pltpu.VMEM((n_grp * 8, 128), F32),
            pltpu.VMEM((TILE, 128), F32),
            block, block, block, block, block, block,
            pltpu.SemaphoreType.DMA((4,)),
            pltpu.SemaphoreType.DMA((3,)),
            pltpu.SemaphoreType.DMA((3,)),
            pltpu.SemaphoreType.DMA((3,)),
        ],
        compiler_params=pltpu.CompilerParams(
            collective_id=0, has_side_effects=True, vmem_limit_bytes=24 * 1024 * 1024
        ),
        name="exchange",
    )(strain.T, pairs.T, half_widths.reshape(1, -1), fir_taps.reshape(1, -1))
    scratch = pltpu.VMEM((2, LINES * BAND, 128), F32)
    return pl.pallas_call(
        correlate_kernel,
        out_shape=jax.ShapeDtypeStruct((1, PMAX, TILE, TILE, LAGS), BF16),
        in_specs=[vmem, vmem],
        out_specs=pl.BlockSpec(memory_space=pl.ANY),
        scratch_shapes=[
            scratch,
            scratch,
            pltpu.VMEM((2, HALF, TILE, TILE, LAGS), BF16),
            pltpu.SemaphoreType.DMA((2,)),
        ],
        compiler_params=pltpu.CompilerParams(vmem_limit_bytes=32 * 1024 * 1024),
        name="correlate",
    )(weights, lines)


def solution(mesh):
    placed = (P(None, "grp"), P(), P("grp"), P())
    return jax.shard_map(
        functools.partial(on_device, mesh.shape["grp"], mesh.shape["rep"]),
        mesh=mesh,
        in_specs=placed,
        out_specs=P(("grp", "rep"), None, None, None, None),
        check_vma=False,
    )
```

time: 460 us -> 32.3 us (0.07)
  local copies, waits for them, and re-layouts: 327 us -> 2.94 us
  waiting for transfers between devices: 70.4 us -> 0 us
  Pallas kernels: 0 us -> 29.2 us
  matrix products: 16.4 us -> 0 us
  between operations: 14 us -> 0.01 us
  starting transfers between devices: 13 us -> 0 us
  blocking collectives: 10.9 us -> 0 us
  other arithmetic: 6.09 us -> 0 us
    gather x7 -> x0, local copies, waits for them, and re-layouts: 247 us -> none  [the longest x3 121 us: normalize(): jnp.take_along_axis(prefix, lower_end, axis=1)]
    all_gather x1 -> x0, waiting for transfers between devices: 63.8 us -> none  [on_device(): piece = lax.all_gather(row_tiles, 'grp', axis=0, tiled=True)]
    concatenate x10 -> x0, local copies, waits for them, and re-layouts: 62.9 us -> none  [the longest x9 62.8 us: correlate(): return jnp.concatenate(pieces, axis=3).astype(jnp.bfloat16)]
    pallas_call x0 -> x2, Pallas kernels: none -> 29.2 us  [the longest x1 24.1 us: on_device(): pl.pallas_call(functools.partial(exchange_kernel, n_grp, n_rep), out_shap...]
    dot_general x10 -> x0, matrix products: 16.4 us -> none  [the longest x8 15.8 us: correlate(): lax.dot_general(flat, shifted.reshape(tile_width * lag_width, length), ((...]
    all_to_all x1 -> x0, starting transfers between devices: 13 us -> none  [on_device(): lax.all_to_all(strain, 'grp', split_axis=0, concat_axis=1, tiled=True)]
    all_gather x1 -> x0, blocking collectives: 10.9 us -> none  [on_device(): row_tiles = lax.all_gather(own[None], 'rep', axis=0, tiled=True)]
    unnamed x77 -> x8, local copies, waits for them, and re-layouts: 10 us -> 2.94 us
  transfers between devices with their start and end apart: 2 -> 0, of which waited for: 2 -> 0; matrix products, arithmetic and copies ran while one was open for 4% -> 0% of each run, Pallas kernels for 0% -> 0%
where the time goes in v2:
time: 32.3 us; the launch traced here: 32.1 us
  Pallas kernels  29.2 us (90%)
  local copies, waits for them, and re-layouts  2.94 us (9%)
    pallas_call x1, Pallas kernels, on_device(): pl.pallas_call(functools.partial(exchange_kernel, n_grp, n_rep), out_shap...  24.1 us
    pallas_call x1, Pallas kernels, on_device(): pl.pallas_call(correlate_kernel, out_shape=jax.ShapeDtypeStruct((1, PMAX,...  5.06 us
    unnamed x8, local copies, waits for them, and re-layouts  2.94 us

profile of v2, /device:TPU:1, one launch (start us, length us, event | category | flops | bytes accessed | tf_op | source)
XLA Modules:
  0.0 32.1 jit_solution(16220017548556217663)
XLA Ops:
  0.0 0.0 copy-start
  0.0 0.9 %copy-done = bf16[10240,6]{0,1:T(8,128)(2,1)S(1)} copy-done((bf16[10240,6]{0,1:T(8,128)(2,1)S(1)}, bf16[10240,6]{0,1:T(8,128)(2,1)}, u32[]{:S(2)}) %copy-start) | copy-done | bytes 122904
  0.9 0.0 copy-start.1
  0.9 0.7 %copy-done.1 = s32[256,8]{0,1:T(8,128)S(1)} copy-done((s32[256,8]{0,1:T(8,128)S(1)}, s32[256,8]{0,1:T(8,128)}, u32[]{:S(2)}) %copy-start.1) | copy-done | bytes 8216
  1.6 0.0 copy-start.2
  1.6 0.7 %copy-done.2 = s32[160]{0:T(256)S(1)} copy-done((s32[160]{0:T(256)S(1)}, s32[160]{0:T(256)}, u32[]{:S(2)}) %copy-start.2) | copy-done | bytes 664
  2.3 0.0 copy-start.3
  2.3 0.7 %copy-done.3 = f32[64]{0:T(128)S(1)} copy-done((f32[64]{0:T(128)S(1)}, f32[64]{0:T(128)}, u32[]{:S(2)}) %copy-start.3) | copy-done | bytes 280
  2.9 24.1 %exchange.1 = (bf16[20,256,256]{2,1,0:T(8,128)(2,1)S(1)}, bf16[2,320,256]{2,1,0:T(8,128)(2,1)S(1)}) custom-call(bf16[6,10240]{1,0:T(8,128)(2,1)S(1)} %bitcast.4, s32[8,256]{1,0:T(8,128)S(1)} %bitcast.5, s32[1,160]{1,0:T(1,128)S(1)} %bitcast.6, f32[1,64]{1,0:T(1,128)S(1)} %bitcast.7), custom_call_target="tpu_custom_call" | custom-call | tf_op jit(solution)/shard_map/exchange/pallas_call | solution.py:300
  27.1 5.1 %correlate.1 = bf16[1,8,40,40,256]{4,3,2,1,0:T(8,128)(2,1)} custom-call(bf16[20,256,256]{2,1,0:T(8,128)(2,1)S(1)} %get-tuple-element.7.w_ref, bf16[2,320,256]{2,1,0:T(8,128)(2,1)S(1)} %get-tuple-element.8.ab_ref), custom_call_target="tpu_custom_call" | custom-call | tf_op jit(solution)/shard_map/correlate/pallas_call | solution.py:328
Async XLA Ops:
  0.0 0.9 %copy-start = (bf16[10240,6]{0,1:T(8,128)(2,1)S(1)}, bf16[10240,6]{0,1:T(8,128)(2,1)}, u32[]{:S(2)}) copy-start(bf16[10240,6]{0,1:T(8,128)(2,1)} %param.4) | copy-start | bytes 368644
  0.9 0.7 %copy-start.1 = (s32[256,8]{0,1:T(8,128)S(1)}, s32[256,8]{0,1:T(8,128)}, u32[]{:S(2)}) copy-start(s32[256,8]{0,1:T(8,128)} %param.7) | copy-start | bytes 24580
  1.6 0.7 %copy-start.2 = (s32[160]{0:T(256)S(1)}, s32[160]{0:T(256)}, u32[]{:S(2)}) copy-start(s32[160]{0:T(256)} %param.6) | copy-start | bytes 1924
  2.3 0.7 %copy-start.3 = (f32[64]{0:T(128)S(1)}, f32[64]{0:T(128)}, u32[]{:S(2)}) copy-start(f32[64]{0:T(128)} %param.5) | copy-start | bytes 772

commit v3 on v2

--- a/solution.py
+++ b/solution.py
@@ -155,8 +155,8 @@
 
 
 def exchange_kernel(
-    n_grp, n_rep, strain_hbm, pairs_hbm, widths_hbm, taps_hbm, w_ref, ab_ref,
-    strain, pairs, widths, taps, rows_f, flat, own_ref,
+    n_grp, n_rep, strain_hbm, pairs_hbm, widths_hbm, taps_hbm, w_ref, ab_ref, first_ref,
+    strain, pairs, widths, taps, rows_f, flat, own_ref, ab_first, sc_a, sc_b,
     send_0, send_1, send_2, got_0, got_1, got_2, in_sems, send_sems, recv_sems, local_sems,
 ):
     me = lax.axis_index("grp")
@@ -258,36 +258,42 @@
             for b in range(3):
                 columns[b].append(white[b])
         white = [jnp.concatenate(column, axis=0).astype(BF16) for column in columns]
-        ab_ref[part, 0:LINES, 0:128] = white[0]
-        ab_ref[part, 0:LINES, 128:256] = white[1]
-        ab_ref[part, LINES : 2 * LINES, 0:128] = white[1]
-        ab_ref[part, LINES : 2 * LINES, 128:256] = white[2]
+        target = (ab_first, ab_ref)[part]
+        target[0:LINES, 0:128] = white[0]
+        target[0:LINES, 128:256] = white[1]
+        target[LINES : 2 * LINES, 0:128] = white[1]
+        target[LINES : 2 * LINES, 128:256] = white[2]
+        if part == 0:
+            correlate_part(ab_first, w_ref, (sc_a, sc_b), first_ref)
 
     for wave in range(3):
         pltpu.make_async_copy(sends[wave].at[others], sends[wave].at[others], send_sems.at[wave]).wait()
 
 
-def correlate_kernel(w_ref, ab_ref, out_ref, sc_a, sc_b, done, sems):
+def correlate_part(lines_ref, w_ref, scratches, done):
     normalizer = 1.0 / math.sqrt(SUMMED)
-    copies = []
-    turn = 0
-    for part in range(2):
-        for at in range(0, TILE, BAND):
-            sc = (sc_a, sc_b)[turn % 2]
-            turn += 1
-            for pair in range(BAND // 2):
-                product = jnp.dot(ab_ref[part], w_ref[at // 2 + pair], preferred_element_type=F32)
-                product = product * normalizer
-                for k in range(2):
-                    for half in range(2):
-                        sc[half, pl.ds(2 * pair + k, LINES, stride=BAND), :] = product[
-                            LINES * half : LINES * (half + 1), 128 * k : 128 * (k + 1)
-                        ]
-            piece = jnp.concatenate([sc[0], sc[1]], axis=1)
-            done[part, :, :, at : at + BAND, :] = piece.reshape(HALF, TILE, BAND, LAGS).astype(BF16)
-        copy = pltpu.make_async_copy(done.at[part], out_ref.at[0, pl.ds(HALF * part, HALF)], sems.at[part])
-        copy.start()
-        copies.append(copy)
+    slots = done.shape[0]
+    lines = slots * TILE
+    for turn, at in enumerate(range(0, TILE, BAND)):
+        sc = scratches[turn % 2]
+        for pair in range(BAND // 2):
+            product = jnp.dot(lines_ref[...], w_ref[at // 2 + pair], preferred_element_type=F32)
+            product = product * normalizer
+            for k in range(2):
+                for half in range(2):
+                    sc[half, pl.ds(2 * pair + k, lines, stride=BAND), :] = product[
+                        lines * half : lines * (half + 1), 128 * k : 128 * (k + 1)
+                    ]
+        piece = jnp.concatenate([sc[0, 0 : lines * BAND, :], sc[1, 0 : lines * BAND, :]], axis=1)
+        done[:, :, at : at + BAND, :] = piece.reshape(slots, TILE, BAND, LAGS).astype(BF16)
+
+
+def correlate_kernel(w_ref, ab_ref, first_ref, out_ref, sc_a, sc_b, done, sems):
+    copies = [pltpu.make_async_copy(first_ref, out_ref.at[0, pl.ds(0, HALF)], sems.at[0])]
+    copies[0].start()
+    correlate_part(ab_ref, w_ref, (sc_a, sc_b), done)
+    copies.append(pltpu.make_async_copy(done, out_ref.at[0, pl.ds(HALF, HALF)], sems.at[1]))
+    copies[1].start()
     for copy in copies:
         copy.wait()
 
@@ -297,14 +303,16 @@
     hbm = pl.BlockSpec(memory_space=pltpu.HBM)
     samples, channels = strain.shape[1], strain.shape[0]
     block = pltpu.VMEM((n_grp, 8, 128), BF16)
-    weights, lines = pl.pallas_call(
+    scratch = pltpu.VMEM((2, LINES * BAND, 128), F32)
+    weights, lines, first = pl.pallas_call(
         functools.partial(exchange_kernel, n_grp, n_rep),
         out_shape=(
             jax.ShapeDtypeStruct((TILE // 2, 256, 256), BF16),
-            jax.ShapeDtypeStruct((2, 2 * LINES, 256), BF16),
+            jax.ShapeDtypeStruct((2 * LINES, 256), BF16),
+            jax.ShapeDtypeStruct((HALF, TILE, TILE, LAGS), BF16),
         ),
         in_specs=[hbm] * 4,
-        out_specs=(vmem, vmem),
+        out_specs=(vmem, vmem, vmem),
         scratch_shapes=[
             pltpu.VMEM((samples, channels), BF16),
             pltpu.VMEM((PMAX, TILES), jnp.int32),
@@ -313,6 +321,8 @@
             pltpu.VMEM((16 * TILE // 128, 8 * TILES // 16, 128), F32),
             pltpu.VMEM((n_grp * 8, 128), F32),
             pltpu.VMEM((TILE, 128), F32),
+            pltpu.VMEM((2 * LINES, 256), BF16),
+            scratch, scratch,
             block, block, block, block, block, block,
             pltpu.SemaphoreType.DMA((4,)),
             pltpu.SemaphoreType.DMA((3,)),
@@ -323,22 +333,24 @@
             collective_id=0, has_side_effects=True, vmem_limit_bytes=24 * 1024 * 1024
         ),
         name="exchange",
-    )(strain.T, pairs.T, half_widths.reshape(1, -1), fir_taps.reshape(1, -1))
-    scratch = pltpu.VMEM((2, LINES * BAND, 128), F32)
+    )(*[
+        pltpu.with_memory_space_constraint(value, pltpu.HBM)
+        for value in (strain.T, pairs.T, half_widths.reshape(1, -1), fir_taps.reshape(1, -1))
+    ])
     return pl.pallas_call(
         correlate_kernel,
         out_shape=jax.ShapeDtypeStruct((1, PMAX, TILE, TILE, LAGS), BF16),
-        in_specs=[vmem, vmem],
+        in_specs=[vmem] * 3,
         out_specs=pl.BlockSpec(memory_space=pl.ANY),
         scratch_shapes=[
             scratch,
             scratch,
-            pltpu.VMEM((2, HALF, TILE, TILE, LAGS), BF16),
+            pltpu.VMEM((HALF, TILE, TILE, LAGS), BF16),
             pltpu.SemaphoreType.DMA((2,)),
         ],
         compiler_params=pltpu.CompilerParams(vmem_limit_bytes=32 * 1024 * 1024),
         name="correlate",
-    )(weights, lines)
+    )(weights, lines, first)
 
 
 def solution(mesh):

time: 32.3 us -> 28 us (0.87)
  local copies, waits for them, and re-layouts: 2.94 us -> 0 us
  Pallas kernels: 29.2 us -> 27.9 us
    unnamed x8 -> x0, local copies, waits for them, and re-layouts: 2.94 us -> none
    pallas_call x1, Pallas kernels: 5.06 us -> 3.46 us  [on_device(): pl.pallas_call(correlate_kernel, out_shape=jax.ShapeDtypeStruct((1, PMAX,...]
where the time goes in v3:
time: 28 us; the launch traced here: 27.9 us
  Pallas kernels  27.9 us (100%)
    pallas_call x1, Pallas kernels, on_device(): pl.pallas_call(functools.partial(exchange_kernel, n_grp, n_rep), out_shap...  24.4 us
    pallas_call x1, Pallas kernels, on_device(): pl.pallas_call(correlate_kernel, out_shape=jax.ShapeDtypeStruct((1, PMAX,...  3.46 us

profile of v3, /device:TPU:1, one launch (start us, length us, event | category | flops | bytes accessed | tf_op | source)
XLA Modules:
  0.0 27.9 jit_solution(16298723079094836942)
XLA Ops:
  0.0 24.4 %exchange.1 = (bf16[20,256,256]{2,1,0:T(8,128)(2,1)S(1)}, bf16[320,256]{1,0:T(8,128)(2,1)S(1)}, bf16[4,40,40,256]{3,2,1,0:T(8,128)(2,1)S(1)}) custom-call(bf16[6,10240]{1,0:T(8,128)(2,1)} %bitcast.4, s32[8,256]{1,0:T(8,128)} %bitcast.5, s32[1,160]{1,0:T(1,128)} %bitcast.6, f32[1,64]{1,0:T(1,128)} %bitcast.7), custom_call_target="tpu_custom_call" | custom-call | tf_op jit(solution)/shard_map/exchange/pallas_call | solution.py:307
  24.4 3.5 %correlate.1 = bf16[1,8,40,40,256]{4,3,2,1,0:T(8,128)(2,1)} custom-call(bf16[20,256,256]{2,1,0:T(8,128)(2,1)S(1)} %get-tuple-element.8.w_ref, bf16[320,256]{1,0:T(8,128)(2,1)S(1)} %get-tuple-element.9.ab_ref, bf16[4,40,40,256]{3,2,1,0:T(8,128)(2,1)S(1)} %get-tuple-element.10.first_ref), custom_call_target="tpu_custom_call" | custom-call | tf_op jit(solution)/shard_map/correlate/pallas_call | solution.py:340

commit v4 on v3

--- a/solution.py
+++ b/solution.py
@@ -44,7 +44,7 @@
     return jnp.concatenate([row, jnp.zeros((1, 128 - row.shape[1]), row.dtype)], axis=1)
 
 
-def pack_messages(n_grp, n_rep, rep, samples, strain, pairs, widths, rows_f, sends):
+def pack_messages(n_grp, n_rep, me, rep, samples, strain, pairs, widths, rows_f, sends):
     groups = TILES // 16
     span = 16 * TILE
     for g in range(groups):
@@ -78,56 +78,85 @@
     own = jnp.dot(one_hot(tile == home), x, preferred_element_type=F32)
     block = jnp.where(upper == 0, own[:, :128], 0.0)
     block = jnp.where(upper == 1, own[:, 128:], block)
-    block = jnp.where(upper == 2, jnp.broadcast_to(widths[0], (rows, 128)), block)
-    block = jnp.where(upper == 3, jnp.broadcast_to(widths[1], (rows, 128)), block)
-    sends[0][...] = block.reshape(n_grp, 8, 128).astype(BF16)
+    sends[0] = block.reshape(n_grp, 8, 128).astype(BF16)
+
+    strips = []
+    for q in range(HALF):
+        for k in range(n_rep):
+            begin, end = TILE * k + 16 * q, min(TILE * k + 16 * q + 16, TILE * (k + 1))
+            if begin < end:
+                strips.append(
+                    jnp.concatenate(
+                        [
+                            jnp.zeros((1, 112), F32),
+                            widths[:, begin:end],
+                            jnp.zeros((1, 16 - end + begin), F32),
+                        ][: 3 if end - begin < 16 else 2],
+                        axis=1,
+                    )
+                )
+            else:
+                strips.append(jnp.zeros((1, 128), F32))
+    strips = jnp.concatenate(strips, axis=0).astype(BF16)
+    spread = iota((rows, HALF * n_rep), 1)
+    in_group = jnp.zeros((rows, HALF * n_rep), F32)
+    for p in range(PMAX):
+        same = listed[:, p : p + 1] == (me * n_rep + spread % n_rep).astype(F32)
+        in_group = jnp.where(same, 1.0, in_group)
+    at_row = iota((rows, HALF * n_rep), 0) % 8 == HALF + spread // n_rep
+    width_part = jnp.dot(
+        jnp.where(at_row, in_group, 0.0).astype(BF16), strips, preferred_element_type=F32
+    )
     for part in range(2):
         ids = jnp.sum(
             jnp.where(slot == sub % HALF + HALF * part, listed, 0.0), axis=1, keepdims=True
         )
         taken = jnp.dot(one_hot(tile.astype(F32) == ids), x, preferred_element_type=F32)
         block = jnp.where(upper < HALF, taken[:, :128], taken[:, 128:])
-        sends[1 + part][...] = block.reshape(n_grp, 8, 128).astype(BF16)
-
-
-def fir_matrix(n_grp, samples, taps):
-    stair = pltpu.roll(jnp.broadcast_to(wide_row(taps), (8, 128)), 0, 1, stride=samples, stride_axis=0)
-    lane = iota((8, 128), 1)
-    zero = jnp.zeros((8, 128), F32)
-    strips = []
-    for tt in range(samples):
-        for block in range(n_grp // 8):
-            shift = samples * 8 * block + tt
-            first, by = shift // 128, shift % 128
-            turned = pltpu.roll(stair, by, 1) if by else stair
-            columns = [zero] * (NT // 128 + 1)
-            columns[first] = jnp.where(lane >= by, turned, 0.0)
-            columns[first + 1] = jnp.where(lane < by, turned, 0.0)
-            strips.append(jnp.concatenate(columns[: NT // 128], axis=1))
-    return split3(jnp.concatenate(strips, axis=0))
+        if part == 0:
+            block = block + width_part
+        sends[1 + part] = block.reshape(n_grp, 8, 128).astype(BF16)
+
+
+def fir_matrix(taps):
+    turned = pltpu.roll(
+        jnp.broadcast_to(wide_row(taps), (128, 128)), 0, 1, stride=1, stride_axis=0
+    )
+    here = iota((128, 128), 1) >= iota((128, 128), 0)
+    both = jnp.concatenate([jnp.where(here, 0.0, turned), jnp.where(here, turned, 0.0)], axis=0)
+    return jnp.concatenate(split3(both), axis=1)
 
 
 def unfold(n_grp, samples, flat, low_row, high_row):
     low = flat[pl.ds(low_row, n_grp, stride=8), :]
     high = flat[pl.ds(high_row, n_grp, stride=8), :]
-    turned = jnp.concatenate([low.T, high.T], axis=0)
+    high_turned = high.T
+    turned = jnp.concatenate([low.T, high_turned], axis=0)
     parts = [turned[TILE * tt : TILE * (tt + 1)] for tt in range(samples)]
-    return jnp.concatenate(parts, axis=1)
-
-
-def filter_and_sum(raw, fir, upper):
-    raw = raw.astype(BF16)
-    filtered = jnp.dot(raw, fir[2], preferred_element_type=F32)
-    filtered = filtered + jnp.dot(raw, fir[1], preferred_element_type=F32)
-    filtered = filtered + jnp.dot(raw, fir[0], preferred_element_type=F32)
-    sizes = split3(jnp.abs(filtered))
-    prefix = jnp.dot(sizes[2], upper, preferred_element_type=F32)
-    prefix = prefix + jnp.dot(sizes[1], upper, preferred_element_type=F32)
-    prefix = prefix + jnp.dot(sizes[0], upper, preferred_element_type=F32)
-    return filtered, prefix
-
-
-def whiten(filtered, prefix, width_f, blocks_out):
+    return jnp.concatenate(parts, axis=1), high_turned[112:128]
+
+
+def filter_and_sum(raw, order, fir, upper):
+    rows = raw.shape[0]
+    timed = jnp.dot(raw.astype(BF16), order, preferred_element_type=F32)
+    blocks = [jnp.zeros((rows, 128), F32)] + [timed[:, 128 * b : 128 * (b + 1)] for b in range(3)]
+    stacked = jnp.concatenate(
+        [jnp.concatenate([blocks[b], blocks[b + 1]], axis=1) for b in range(3)], axis=0
+    )
+    product = jnp.dot(stacked.astype(BF16), fir, preferred_element_type=F32)
+    filtered = product[:, 256:384] + product[:, 128:256] + product[:, 0:128]
+    size = jnp.abs(filtered)
+    high = size.astype(BF16).astype(F32)
+    pieces = jnp.concatenate([high, size - high], axis=1).astype(BF16)
+    sums = jnp.dot(pieces, upper, preferred_element_type=F32)
+    prefix = [sums[0:rows]]
+    for b in (1, 2):
+        before = jnp.broadcast_to(prefix[b - 1][:, 127:128], (rows, 128))
+        prefix.append(sums[rows * b : rows * (b + 1)] + before)
+    return [filtered[rows * b : rows * (b + 1)] for b in range(3)], prefix
+
+
+def whiten(filtered, blocks, width_f, blocks_out):
     lane = iota((TILE, 128), 1)
     width_f = jnp.broadcast_to(width_f, (TILE, 128))
     width = width_f.astype(jnp.int32)
@@ -135,9 +164,8 @@
     down = lane - width - 1
     up_at, up_block = up & 127, up >> 7
     down_at, down_block = down & 127, down >> 7
-    blocks = [prefix[:, 128 * b : 128 * (b + 1)] for b in range(3)]
     ups = [jnp.take_along_axis(block, up_at, axis=1) for block in blocks]
-    downs = [jnp.take_along_axis(block, down_at, axis=1) for block in blocks]
+    downs = [jnp.take_along_axis(block, down_at, axis=1) for block in blocks[:blocks_out]]
     total = jnp.broadcast_to(blocks[2][:, 127:128], (TILE, 128))
     scale = 1.0 / (2.0 * width_f + 1.0)
     results = []
@@ -150,18 +178,20 @@
         if b >= 2:
             begin = jnp.where(down_block == -2, downs[b - 2], begin)
         level = (end - begin) * scale
-        results.append(filtered[:, 128 * b : 128 * (b + 1)] / (level + 1e-05))
+        results.append(filtered[b] / (level + 1e-05))
     return results
 
 
 def exchange_kernel(
     n_grp, n_rep, strain_hbm, pairs_hbm, widths_hbm, taps_hbm, w_ref, ab_ref, first_ref,
     strain, pairs, widths, taps, rows_f, flat, own_ref, ab_first, sc_a, sc_b,
-    send_0, send_1, send_2, got_0, got_1, got_2, in_sems, send_sems, recv_sems, local_sems,
+    sends, gots, in_sems, send_sems, recv_sems, local_sems,
 ):
     me = lax.axis_index("grp")
     rep = lax.axis_index("rep")
     samples = NT // n_grp
+    middle = n_grp // 2
+    near = (SUMMED + 160 + samples - 1) // samples
     barrier = pltpu.get_barrier_semaphore()
     loads = [
         pltpu.make_async_copy(source, target, in_sems.at[k])
@@ -171,66 +201,82 @@
     ]
     for load in loads:
         load.start()
-
-    def greet(k, carry):
+    for k in range(1, n_grp):
         pl.semaphore_signal(
             barrier, inc=1, device_id={"grp": lax.rem(me + k, n_grp)}, device_id_type=MESH
         )
-        return carry
-
-    lax.fori_loop(1, n_grp, greet, 0)
     for load in loads:
         load.wait()
 
-    sends = (send_0, send_1, send_2)
-    gots = (got_0, got_1, got_2)
-    count = widths.shape[1]
-    width_rows = [widths[:, 0:128].astype(F32), wide_row(widths[:, 128:count].astype(F32))]
-    pack_messages(n_grp, n_rep, rep, samples, strain, pairs[...], width_rows, rows_f, sends)
-
+    width_row = widths[...].astype(F32)
+    pack_messages(n_grp, n_rep, me, rep, samples, strain, pairs[...], width_row, rows_f, sends)
+
+    late = me >= middle
     pl.semaphore_wait(barrier, n_grp - 1)
-    for wave in range(3):
-
-        def ship(k, carry):
-            half = (k + 1) // 2
-            to = lax.rem(me + jnp.where(k % 2 == 1, half, n_grp - half), n_grp)
+
+    def ship(n, carry):
+        block = n // middle
+        wave = jnp.where(late, lax.rem(block, 3), block // 2)
+        side = jnp.where(late, block // 3, lax.rem(block, 2))
+        k = lax.rem(n, middle)
+        half = (k + 1) // 2
+        step = jnp.where(lax.rem(k, 2) == 1, half, middle - half)
+        to = middle * side + lax.rem(me + step, middle)
+
+        @pl.when((to != me) & ((wave > 0) | (me < near)))
+        def _():
             pltpu.make_async_remote_copy(
-                src_ref=sends[wave].at[to],
-                dst_ref=gots[wave].at[me],
+                src_ref=sends.at[wave, to],
+                dst_ref=gots.at[wave, me],
                 send_sem=send_sems.at[wave],
                 recv_sem=recv_sems.at[wave],
                 device_id={"grp": to},
                 device_id_type=MESH,
             ).start()
-            return carry
-
-        lax.fori_loop(1, n_grp, ship, 0)
-        pltpu.make_async_copy(sends[wave].at[me], gots[wave].at[me], local_sems.at[wave]).start()
-
-    others = pl.ds(0, n_grp - 1)
-
-    def arrive(wave):
-        pltpu.make_async_copy(sends[wave].at[me], gots[wave].at[me], local_sems.at[wave]).wait()
-        pltpu.make_async_copy(gots[wave].at[others], gots[wave].at[others], recv_sems.at[wave]).wait()
-        flat[...] = gots[wave][...].astype(F32).reshape(n_grp * 8, 128)
-
-    fir = fir_matrix(n_grp, samples, taps[...])
-    upper = one_hot(iota((NT, NT), 0) <= iota((NT, NT), 1))
+
+        return carry
+
+    lax.fori_loop(0, 6 * middle, ship, 0)
+    local = [
+        pltpu.make_async_copy(sends.at[wave, me], gots.at[wave, me], local_sems.at[wave])
+        for wave in range(3)
+    ]
+    for copy in local:
+        copy.start()
+
+    def await_blocks(buffer, sem, wave, count):
+        span = buffer.at[wave, pl.ds(0, count)]
+        pltpu.make_async_copy(span, span, sem.at[wave]).wait()
+
+    fir = fir_matrix(taps[...])
+    upper = one_hot(iota((256, 128), 0) % 128 <= iota((256, 128), 1))
+    arrived = iota((NT, NT), 0)
+    order = one_hot(iota((NT, NT), 1) == samples * (arrived % n_grp) + arrived // n_grp)
     tile = me * n_rep + rep
     mine = jnp.where(iota((PMAX, TILES), 1) == tile, pairs[...], 0)
     ids = jnp.sum(mine.astype(F32), axis=1, keepdims=True)
-    ids = jnp.concatenate([ids, jnp.full((PMAX, 1), tile, jnp.int32).astype(F32)], axis=0)
-    spot = iota((2 * PMAX, TILES), 1)
-    hot = one_hot((n_rep * (spot % n_grp) + spot // n_grp).astype(F32) == ids)
-
-    arrive(0)
-    turned = jnp.concatenate(
-        [flat[pl.ds(2, n_grp, stride=8), :].T, flat[pl.ds(3, n_grp, stride=8), :].T], axis=0
-    )
-    turned = jnp.concatenate([turned[TILE * k : TILE * (k + 1)] for k in range(n_rep)], axis=1)
-    spans = lax.dot_general(turned.astype(BF16), hot, NT_DIMS, preferred_element_type=F32)
-    filtered, prefix = filter_and_sum(unfold(n_grp, samples, flat, 0, 1), fir, upper)
-    own = whiten(filtered, prefix, spans[:, PMAX : PMAX + 1], 1)[0].astype(BF16).astype(F32)
+    group = iota((PMAX, n_grp), 1).astype(F32) * n_rep
+    hot = one_hot((ids >= group) & (ids < group + n_rep))
+    count = widths.shape[1]
+    width_at = iota((TILE, count), 1) == iota((TILE, count), 0) + TILE * rep
+    own_width = jnp.sum(
+        jnp.where(width_at, jnp.broadcast_to(width_row, (TILE, count)), 0.0), axis=1, keepdims=True
+    )
+
+    local[0].wait()
+
+    @pl.when(me < near)
+    def _():
+        await_blocks(gots, recv_sems, 0, near - 1)
+
+    @pl.when(me >= near)
+    def _():
+        await_blocks(gots, recv_sems, 0, near)
+
+    flat[0 : near * 8, :] = gots[0, 0:near].astype(F32).reshape(near * 8, 128)
+    flat[near * 8 :, :] = jnp.zeros(((n_grp - near) * 8, 128), F32)
+    filtered, prefix = filter_and_sum(unfold(n_grp, samples, flat, 0, 1)[0], order, fir, upper)
+    own = whiten(filtered, prefix, own_width, 1)[0].astype(BF16).astype(F32)
     own_ref[...] = jnp.take_along_axis(own, 127 - iota((TILE, 128), 1), axis=1)
     later = iota((128, 128), 1) > iota((128, 128), 0)
 
@@ -242,19 +288,31 @@
             w_ref[pair, 128:256, 128 * k : 128 * (k + 1)] = jnp.where(later, turned, 0.0).astype(BF16)
         return carry
 
-    lax.fori_loop(0, TILE // 2, toeplitz, 0)
+    lax.fori_loop(0, TILE // 2, toeplitz, 0, unroll=4)
 
     for part in range(2):
-        arrive(1 + part)
-        raw = jnp.concatenate(
-            [unfold(n_grp, samples, flat, slot, HALF + slot) for slot in range(HALF)], axis=0
-        )
-        filtered, prefix = filter_and_sum(raw, fir, upper)
+        local[1 + part].wait()
+        await_blocks(gots, recv_sems, 1 + part, n_grp - 1)
+        flat[...] = gots[1 + part].astype(F32).reshape(n_grp * 8, 128)
+        raws, tails = [], []
+        for slot in range(HALF):
+            raw, tail = unfold(n_grp, samples, flat, slot, HALF + slot)
+            raws.append(raw)
+            tails.append(tail)
+        if part == 0:
+            turned = jnp.concatenate([tails[0], tails[1], tails[2][:8]], axis=0)
+            spans = lax.dot_general(turned.astype(BF16), hot, NT_DIMS, preferred_element_type=F32)
+        filtered, prefix = filter_and_sum(jnp.concatenate(raws, axis=0), order, fir, upper)
         columns = [[], [], []]
         for slot in range(HALF):
             rows = slice(TILE * slot, TILE * (slot + 1))
             at = HALF * part + slot
-            white = whiten(filtered[rows], prefix[rows], spans[:, at : at + 1], 3)
+            white = whiten(
+                [block[rows] for block in filtered],
+                [block[rows] for block in prefix],
+                spans[:, at : at + 1],
+                3,
+            )
             for b in range(3):
                 columns[b].append(white[b])
         white = [jnp.concatenate(column, axis=0).astype(BF16) for column in columns]
@@ -266,8 +324,12 @@
         if part == 0:
             correlate_part(ab_first, w_ref, (sc_a, sc_b), first_ref)
 
-    for wave in range(3):
-        pltpu.make_async_copy(sends[wave].at[others], sends[wave].at[others], send_sems.at[wave]).wait()
+    @pl.when(me < near)
+    def _():
+        await_blocks(sends, send_sems, 0, n_grp - 1)
+
+    for wave in range(1, 3):
+        await_blocks(sends, send_sems, wave, n_grp - 1)
 
 
 def correlate_part(lines_ref, w_ref, scratches, done):
@@ -302,7 +364,7 @@
     vmem = pl.BlockSpec(memory_space=pltpu.VMEM)
     hbm = pl.BlockSpec(memory_space=pltpu.HBM)
     samples, channels = strain.shape[1], strain.shape[0]
-    block = pltpu.VMEM((n_grp, 8, 128), BF16)
+    block = pltpu.VMEM((3, n_grp, 8, 128), BF16)
     scratch = pltpu.VMEM((2, LINES * BAND, 128), F32)
     weights, lines, first = pl.pallas_call(
         functools.partial(exchange_kernel, n_grp, n_rep),
@@ -323,7 +385,7 @@
             pltpu.VMEM((TILE, 128), F32),
             pltpu.VMEM((2 * LINES, 256), BF16),
             scratch, scratch,
-            block, block, block, block, block, block,
+            block, block,
             pltpu.SemaphoreType.DMA((4,)),
             pltpu.SemaphoreType.DMA((3,)),
             pltpu.SemaphoreType.DMA((3,)),

time: 28 us -> 26.9 us (0.961)
  Pallas kernels: 27.9 us -> 26.7 us
    pallas_call x1, Pallas kernels: 24.4 us -> 23.2 us  [on_device(): pl.pallas_call(functools.partial(exchange_kernel, n_grp, n_rep), out_shap...]
where the time goes in v4:
time: 26.9 us; the launch traced here: 26.7 us
  Pallas kernels  26.7 us (99%)
    pallas_call x1, Pallas kernels, on_device(): pl.pallas_call(functools.partial(exchange_kernel, n_grp, n_rep), out_shap...  23.2 us
    pallas_call x1, Pallas kernels, on_device(): pl.pallas_call(correlate_kernel, out_shape=jax.ShapeDtypeStruct((1, PMAX,...  3.46 us

profile of v4, /device:TPU:1, one launch (start us, length us, event | category | flops | bytes accessed | tf_op | source)
XLA Modules:
  0.0 26.7 jit_solution(326427008331998062)
XLA Ops:
  0.0 23.2 %exchange.1 = (bf16[20,256,256]{2,1,0:T(8,128)(2,1)S(1)}, bf16[320,256]{1,0:T(8,128)(2,1)S(1)}, bf16[4,40,40,256]{3,2,1,0:T(8,128)(2,1)S(1)}) custom-call(bf16[6,10240]{1,0:T(8,128)(2,1)} %bitcast.4, s32[8,256]{1,0:T(8,128)} %bitcast.5, s32[1,160]{1,0:T(1,128)} %bitcast.6, f32[1,64]{1,0:T(1,128)} %bitcast.7), custom_call_target="tpu_custom_call" | custom-call | tf_op jit(solution)/shard_map/exchange/pallas_call | solution.py:369
  23.3 3.5 %correlate.1 = bf16[1,8,40,40,256]{4,3,2,1,0:T(8,128)(2,1)} custom-call(bf16[20,256,256]{2,1,0:T(8,128)(2,1)S(1)} %get-tuple-element.8.w_ref, bf16[320,256]{1,0:T(8,128)(2,1)S(1)} %get-tuple-element.9.ab_ref, bf16[4,40,40,256]{3,2,1,0:T(8,128)(2,1)S(1)} %get-tuple-element.10.first_ref), custom_call_target="tpu_custom_call" | custom-call | tf_op jit(solution)/shard_map/correlate/pallas_call | solution.py:402

commit v5 on v4

--- a/solution.py
+++ b/solution.py
@@ -18,6 +18,7 @@
 HALF = PMAX // 2
 LINES = HALF * TILE
 BAND = 8
+PIECES = 2
 F32 = jnp.float32
 BF16 = jnp.bfloat16
 NT_DIMS = (((1,), (1,)), ((), ()))
@@ -211,19 +212,18 @@
     width_row = widths[...].astype(F32)
     pack_messages(n_grp, n_rep, me, rep, samples, strain, pairs[...], width_row, rows_f, sends)
 
-    late = me >= middle
     pl.semaphore_wait(barrier, n_grp - 1)
 
     def ship(n, carry):
         block = n // middle
-        wave = jnp.where(late, lax.rem(block, 3), block // 2)
-        side = jnp.where(late, block // 3, lax.rem(block, 2))
+        wave = jnp.where(me < near, 0, 1) + block // 2
+        side = lax.rem(block, 2)
         k = lax.rem(n, middle)
         half = (k + 1) // 2
         step = jnp.where(lax.rem(k, 2) == 1, half, middle - half)
         to = middle * side + lax.rem(me + step, middle)
 
-        @pl.when((to != me) & ((wave > 0) | (me < near)))
+        @pl.when(to != me)
         def _():
             pltpu.make_async_remote_copy(
                 src_ref=sends.at[wave, to],
@@ -236,7 +236,7 @@
 
         return carry
 
-    lax.fori_loop(0, 6 * middle, ship, 0)
+    lax.fori_loop(0, jnp.where(me < near, 6 * middle, 4 * middle), ship, 0)
     local = [
         pltpu.make_async_copy(sends.at[wave, me], gots.at[wave, me], local_sems.at[wave])
         for wave in range(3)
@@ -317,12 +317,16 @@
                 columns[b].append(white[b])
         white = [jnp.concatenate(column, axis=0).astype(BF16) for column in columns]
         target = (ab_first, ab_ref)[part]
-        target[0:LINES, 0:128] = white[0]
-        target[0:LINES, 128:256] = white[1]
-        target[LINES : 2 * LINES, 0:128] = white[1]
-        target[LINES : 2 * LINES, 128:256] = white[2]
+        pieces = target.shape[0]
+        size = LINES // pieces
+        for piece in range(pieces):
+            low, mid, high = [column[size * piece : size * (piece + 1)] for column in white]
+            target[piece, 0:size, 0:128] = low
+            target[piece, 0:size, 128:256] = mid
+            target[piece, size : 2 * size, 0:128] = mid
+            target[piece, size : 2 * size, 128:256] = high
         if part == 0:
-            correlate_part(ab_first, w_ref, (sc_a, sc_b), first_ref)
+            correlate_part(ab_first.at[0], w_ref, (sc_a, sc_b), first_ref)
 
     @pl.when(me < near)
     def _():
@@ -353,9 +357,17 @@
 def correlate_kernel(w_ref, ab_ref, first_ref, out_ref, sc_a, sc_b, done, sems):
     copies = [pltpu.make_async_copy(first_ref, out_ref.at[0, pl.ds(0, HALF)], sems.at[0])]
     copies[0].start()
-    correlate_part(ab_ref, w_ref, (sc_a, sc_b), done)
-    copies.append(pltpu.make_async_copy(done, out_ref.at[0, pl.ds(HALF, HALF)], sems.at[1]))
-    copies[1].start()
+    pieces = ab_ref.shape[0]
+    size = HALF // pieces
+    for piece in range(pieces):
+        target = done.at[pl.ds(size * piece, size)]
+        correlate_part(ab_ref.at[piece], w_ref, (sc_a, sc_b), target)
+        copies.append(
+            pltpu.make_async_copy(
+                target, out_ref.at[0, pl.ds(HALF + size * piece, size)], sems.at[1 + piece]
+            )
+        )
+        copies[-1].start()
     for copy in copies:
         copy.wait()
 
@@ -370,7 +382,7 @@
         functools.partial(exchange_kernel, n_grp, n_rep),
         out_shape=(
             jax.ShapeDtypeStruct((TILE // 2, 256, 256), BF16),
-            jax.ShapeDtypeStruct((2 * LINES, 256), BF16),
+            jax.ShapeDtypeStruct((PIECES, 2 * LINES // PIECES, 256), BF16),
             jax.ShapeDtypeStruct((HALF, TILE, TILE, LAGS), BF16),
         ),
         in_specs=[hbm] * 4,
@@ -383,7 +395,7 @@
             pltpu.VMEM((16 * TILE // 128, 8 * TILES // 16, 128), F32),
             pltpu.VMEM((n_grp * 8, 128), F32),
             pltpu.VMEM((TILE, 128), F32),
-            pltpu.VMEM((2 * LINES, 256), BF16),
+            pltpu.VMEM((1, 2 * LINES, 256), BF16),
             scratch, scratch,
             block, block,
             pltpu.SemaphoreType.DMA((4,)),
@@ -408,7 +420,7 @@
             scratch,
             scratch,
             pltpu.VMEM((HALF, TILE, TILE, LAGS), BF16),
-            pltpu.SemaphoreType.DMA((2,)),
+            pltpu.SemaphoreType.DMA((1 + PIECES,)),
         ],
         compiler_params=pltpu.CompilerParams(vmem_limit_bytes=32 * 1024 * 1024),
         name="correlate",

time: 26.9 us -> 26.1 us (0.970)
  Pallas kernels: 26.7 us -> 26 us
    pallas_call x1, Pallas kernels: 3.46 us -> 3.1 us  [on_device(): pl.pallas_call(correlate_kernel, out_shape=jax.ShapeDtypeStruct((1, PMAX,...]
    pallas_call x1, Pallas kernels: 23.2 us -> 22.9 us  [on_device(): pl.pallas_call(functools.partial(exchange_kernel, n_grp, n_rep), out_shap...]
where the time goes in v5:
time: 26.1 us; the launch traced here: 26 us
  Pallas kernels  26 us (100%)
    pallas_call x1, Pallas kernels, on_device(): pl.pallas_call(functools.partial(exchange_kernel, n_grp, n_rep), out_shap...  22.9 us
    pallas_call x1, Pallas kernels, on_device(): pl.pallas_call(correlate_kernel, out_shape=jax.ShapeDtypeStruct((1, PMAX,...  3.1 us

profile of v5, /device:TPU:1, one launch (start us, length us, event | category | flops | bytes accessed | tf_op | source)
XLA Modules:
  0.0 26.0 jit_solution(6934359854541756893)
XLA Ops:
  0.0 22.9 %exchange.1 = (bf16[20,256,256]{2,1,0:T(8,128)(2,1)S(1)}, bf16[2,160,256]{2,1,0:T(8,128)(2,1)S(1)}, bf16[4,40,40,256]{3,2,1,0:T(8,128)(2,1)S(1)}) custom-call(bf16[6,10240]{1,0:T(8,128)(2,1)} %bitcast.4, s32[8,256]{1,0:T(8,128)} %bitcast.5, s32[1,160]{1,0:T(1,128)} %bitcast.6, f32[1,64]{1,0:T(1,128)} %bitcast.7), custom_call_target="tpu_custom_call" | custom-call | tf_op jit(solution)/shard_map/exchange/pallas_call | solution.py:381
  22.9 3.1 %correlate.1 = bf16[1,8,40,40,256]{4,3,2,1,0:T(8,128)(2,1)} custom-call(bf16[20,256,256]{2,1,0:T(8,128)(2,1)S(1)} %get-tuple-element.8.w_ref, bf16[2,160,256]{2,1,0:T(8,128)(2,1)S(1)} %get-tuple-element.9.ab_ref, bf16[4,40,40,256]{3,2,1,0:T(8,128)(2,1)S(1)} %get-tuple-element.10.first_ref), custom_call_target="tpu_custom_call" | custom-call | tf_op jit(solution)/shard_map/correlate/pallas_call | solution.py:414

commit v6 on v5

--- a/solution.py
+++ b/solution.py
@@ -45,7 +45,7 @@
     return jnp.concatenate([row, jnp.zeros((1, 128 - row.shape[1]), row.dtype)], axis=1)
 
 
-def pack_messages(n_grp, n_rep, me, rep, samples, strain, pairs, widths, rows_f, sends):
+def pack_messages(n_grp, n_rep, me, rep, samples, strain, pairs, widths, rows_f, send_own, sends):
     groups = TILES // 16
     span = 16 * TILE
     for g in range(groups):
@@ -76,10 +76,11 @@
     sub = iota((rows, PMAX), 0) % 8
     slot = iota((rows, PMAX), 1)
     upper = iota((rows, 128), 0) % 8
-    own = jnp.dot(one_hot(tile == home), x, preferred_element_type=F32)
-    block = jnp.where(upper == 0, own[:, :128], 0.0)
-    block = jnp.where(upper == 1, own[:, 128:], block)
-    sends[0] = block.reshape(n_grp, 8, 128).astype(BF16)
+    pair_row = iota((2 * n_grp, TILES), 0)
+    pair_home = (pair_row // 2) * n_rep + rep
+    own = jnp.dot(one_hot(tile[: 2 * n_grp] == pair_home), x, preferred_element_type=F32)
+    block = jnp.where(iota((2 * n_grp, 128), 0) % 2 == 0, own[:, :128], own[:, 128:])
+    send_own[...] = block.reshape(n_grp, 2, 128).astype(BF16)
 
     strips = []
     for q in range(HALF):
@@ -116,7 +117,7 @@
         block = jnp.where(upper < HALF, taken[:, :128], taken[:, 128:])
         if part == 0:
             block = block + width_part
-        sends[1 + part] = block.reshape(n_grp, 8, 128).astype(BF16)
+        sends[part] = block.reshape(n_grp, 8, 128).astype(BF16)
 
 
 def fir_matrix(taps):
@@ -128,9 +129,9 @@
     return jnp.concatenate(split3(both), axis=1)
 
 
-def unfold(n_grp, samples, flat, low_row, high_row):
-    low = flat[pl.ds(low_row, n_grp, stride=8), :]
-    high = flat[pl.ds(high_row, n_grp, stride=8), :]
+def unfold(n_grp, samples, flat, low_row, high_row, stride=8):
+    low = flat[pl.ds(low_row, n_grp, stride=stride), :]
+    high = flat[pl.ds(high_row, n_grp, stride=stride), :]
     high_turned = high.T
     turned = jnp.concatenate([low.T, high_turned], axis=0)
     parts = [turned[TILE * tt : TILE * (tt + 1)] for tt in range(samples)]
@@ -186,7 +187,7 @@
 def exchange_kernel(
     n_grp, n_rep, strain_hbm, pairs_hbm, widths_hbm, taps_hbm, w_ref, ab_ref, first_ref,
     strain, pairs, widths, taps, rows_f, flat, own_ref, ab_first, sc_a, sc_b,
-    sends, gots, in_sems, send_sems, recv_sems, local_sems,
+    send_own, got_own, sends, gots, in_sems, send_sems, recv_sems, local_sems,
 ):
     me = lax.axis_index("grp")
     rep = lax.axis_index("rep")
@@ -210,7 +211,7 @@
         load.wait()
 
     width_row = widths[...].astype(F32)
-    pack_messages(n_grp, n_rep, me, rep, samples, strain, pairs[...], width_row, rows_f, sends)
+    pack_messages(n_grp, n_rep, me, rep, samples, strain, pairs[...], width_row, rows_f, send_own, sends)
 
     pl.semaphore_wait(barrier, n_grp - 1)
 
@@ -218,35 +219,41 @@
         block = n // middle
         wave = jnp.where(me < near, 0, 1) + block // 2
         side = lax.rem(block, 2)
-        k = lax.rem(n, middle)
-        half = (k + 1) // 2
-        step = jnp.where(lax.rem(k, 2) == 1, half, middle - half)
-        to = middle * side + lax.rem(me + step, middle)
-
-        @pl.when(to != me)
-        def _():
+        to = middle * side + lax.rem(me + lax.rem(n, middle), middle)
+
+        def send(source, target):
             pltpu.make_async_remote_copy(
-                src_ref=sends.at[wave, to],
-                dst_ref=gots.at[wave, me],
+                src_ref=source,
+                dst_ref=target,
                 send_sem=send_sems.at[wave],
                 recv_sem=recv_sems.at[wave],
                 device_id={"grp": to},
                 device_id_type=MESH,
             ).start()
 
+        @pl.when((to != me) & (wave == 0))
+        def _():
+            send(send_own.at[to], got_own.at[me])
+
+        @pl.when((to != me) & (wave > 0))
+        def _():
+            at = jnp.maximum(wave - 1, 0)
+            send(sends.at[at, to], gots.at[at, me])
+
         return carry
 
     lax.fori_loop(0, jnp.where(me < near, 6 * middle, 4 * middle), ship, 0)
-    local = [
-        pltpu.make_async_copy(sends.at[wave, me], gots.at[wave, me], local_sems.at[wave])
-        for wave in range(3)
-    ]
+    local = [pltpu.make_async_copy(send_own.at[me], got_own.at[me], local_sems.at[0])]
+    for wave in range(2):
+        local.append(
+            pltpu.make_async_copy(sends.at[wave, me], gots.at[wave, me], local_sems.at[1 + wave])
+        )
     for copy in local:
         copy.start()
 
-    def await_blocks(buffer, sem, wave, count):
-        span = buffer.at[wave, pl.ds(0, count)]
-        pltpu.make_async_copy(span, span, sem.at[wave]).wait()
+    def await_blocks(buffer, sem, count):
+        span = buffer.at[pl.ds(0, count)]
+        pltpu.make_async_copy(span, span, sem).wait()
 
     fir = fir_matrix(taps[...])
     upper = one_hot(iota((256, 128), 0) % 128 <= iota((256, 128), 1))
@@ -267,15 +274,15 @@
 
     @pl.when(me < near)
     def _():
-        await_blocks(gots, recv_sems, 0, near - 1)
+        await_blocks(got_own, recv_sems.at[0], near - 1)
 
     @pl.when(me >= near)
     def _():
-        await_blocks(gots, recv_sems, 0, near)
-
-    flat[0 : near * 8, :] = gots[0, 0:near].astype(F32).reshape(near * 8, 128)
-    flat[near * 8 :, :] = jnp.zeros(((n_grp - near) * 8, 128), F32)
-    filtered, prefix = filter_and_sum(unfold(n_grp, samples, flat, 0, 1)[0], order, fir, upper)
+        await_blocks(got_own, recv_sems.at[0], near)
+
+    flat[0 : near * 2, :] = got_own[0:near].astype(F32).reshape(near * 2, 128)
+    flat[near * 2 : n_grp * 2, :] = jnp.zeros(((n_grp - near) * 2, 128), F32)
+    filtered, prefix = filter_and_sum(unfold(n_grp, samples, flat, 0, 1, 2)[0], order, fir, upper)
     own = whiten(filtered, prefix, own_width, 1)[0].astype(BF16).astype(F32)
     own_ref[...] = jnp.take_along_axis(own, 127 - iota((TILE, 128), 1), axis=1)
     later = iota((128, 128), 1) > iota((128, 128), 0)
@@ -292,8 +299,8 @@
 
     for part in range(2):
         local[1 + part].wait()
-        await_blocks(gots, recv_sems, 1 + part, n_grp - 1)
-        flat[...] = gots[1 + part].astype(F32).reshape(n_grp * 8, 128)
+        await_blocks(gots.at[part], recv_sems.at[1 + part], n_grp - 1)
+        flat[...] = gots[part].astype(F32).reshape(n_grp * 8, 128)
         raws, tails = [], []
         for slot in range(HALF):
             raw, tail = unfold(n_grp, samples, flat, slot, HALF + slot)
@@ -330,10 +337,10 @@
 
     @pl.when(me < near)
     def _():
-        await_blocks(sends, send_sems, 0, n_grp - 1)
-
-    for wave in range(1, 3):
-        await_blocks(sends, send_sems, wave, n_grp - 1)
+        await_blocks(send_own, send_sems.at[0], n_grp - 1)
+
+    for wave in range(2):
+        await_blocks(sends.at[wave], send_sems.at[1 + wave], n_grp - 1)
 
 
 def correlate_part(lines_ref, w_ref, scratches, done):
@@ -376,7 +383,8 @@
     vmem = pl.BlockSpec(memory_space=pltpu.VMEM)
     hbm = pl.BlockSpec(memory_space=pltpu.HBM)
     samples, channels = strain.shape[1], strain.shape[0]
-    block = pltpu.VMEM((3, n_grp, 8, 128), BF16)
+    own_block = pltpu.VMEM((n_grp, 2, 128), BF16)
+    block = pltpu.VMEM((2, n_grp, 8, 128), BF16)
     scratch = pltpu.VMEM((2, LINES * BAND, 128), F32)
     weights, lines, first = pl.pallas_call(
         functools.partial(exchange_kernel, n_grp, n_rep),
@@ -397,7 +405,7 @@
             pltpu.VMEM((TILE, 128), F32),
             pltpu.VMEM((1, 2 * LINES, 256), BF16),
             scratch, scratch,
-            block, block,
+            own_block, own_block, block, block,
             pltpu.SemaphoreType.DMA((4,)),
             pltpu.SemaphoreType.DMA((3,)),
             pltpu.SemaphoreType.DMA((3,)),

time: 26.1 us -> 25.9 us (level)
  no operation moved by 1% of the time
where the time goes in v6:
time: 25.9 us; the launch traced here: 25.8 us
  Pallas kernels  25.8 us (100%)
    pallas_call x1, Pallas kernels, on_device(): pl.pallas_call(functools.partial(exchange_kernel, n_grp, n_rep), out_shap...  22.7 us
    pallas_call x1, Pallas kernels, on_device(): pl.pallas_call(correlate_kernel, out_shape=jax.ShapeDtypeStruct((1, PMAX,...  3.1 us

profile of v6, /device:TPU:1, one launch (start us, length us, event | category | flops | bytes accessed | tf_op | source)
XLA Modules:
  0.0 25.8 jit_solution(13325342087587874576)
XLA Ops:
  0.0 22.7 %exchange.1 = (bf16[20,256,256]{2,1,0:T(8,128)(2,1)S(1)}, bf16[2,160,256]{2,1,0:T(8,128)(2,1)S(1)}, bf16[4,40,40,256]{3,2,1,0:T(8,128)(2,1)S(1)}) custom-call(bf16[6,10240]{1,0:T(8,128)(2,1)} %bitcast.4, s32[8,256]{1,0:T(8,128)} %bitcast.5, s32[1,160]{1,0:T(1,128)} %bitcast.6, f32[1,64]{1,0:T(1,128)} %bitcast.7), custom_call_target="tpu_custom_call" | custom-call | tf_op jit(solution)/shard_map/exchange/pallas_call | solution.py:389
  22.7 3.1 %correlate.1 = bf16[1,8,40,40,256]{4,3,2,1,0:T(8,128)(2,1)} custom-call(bf16[20,256,256]{2,1,0:T(8,128)(2,1)S(1)} %get-tuple-element.8.w_ref, bf16[2,160,256]{2,1,0:T(8,128)(2,1)S(1)} %get-tuple-element.9.ab_ref, bf16[4,40,40,256]{3,2,1,0:T(8,128)(2,1)S(1)} %get-tuple-element.10.first_ref), custom_call_target="tpu_custom_call" | custom-call | tf_op jit(solution)/shard_map/correlate/pallas_call | solution.py:422

commit v7 on v6

--- a/solution.py
+++ b/solution.py
@@ -215,34 +215,31 @@
 
     pl.semaphore_wait(barrier, n_grp - 1)
 
-    def ship(n, carry):
-        block = n // middle
-        wave = jnp.where(me < near, 0, 1) + block // 2
-        side = lax.rem(block, 2)
-        to = middle * side + lax.rem(me + lax.rem(n, middle), middle)
-
-        def send(source, target):
-            pltpu.make_async_remote_copy(
-                src_ref=source,
-                dst_ref=target,
-                send_sem=send_sems.at[wave],
-                recv_sem=recv_sems.at[wave],
-                device_id={"grp": to},
-                device_id_type=MESH,
-            ).start()
-
-        @pl.when((to != me) & (wave == 0))
-        def _():
-            send(send_own.at[to], got_own.at[me])
-
-        @pl.when((to != me) & (wave > 0))
-        def _():
-            at = jnp.maximum(wave - 1, 0)
-            send(sends.at[at, to], gots.at[at, me])
-
-        return carry
-
-    lax.fori_loop(0, jnp.where(me < near, 6 * middle, 4 * middle), ship, 0)
+    def ship(source, target, wave):
+        def step(n, carry):
+            to = middle * (n // middle) + lax.rem(me + lax.rem(n, middle), middle)
+
+            @pl.when(to != me)
+            def _():
+                pltpu.make_async_remote_copy(
+                    src_ref=source.at[to],
+                    dst_ref=target.at[me],
+                    send_sem=send_sems.at[wave],
+                    recv_sem=recv_sems.at[wave],
+                    device_id={"grp": to},
+                    device_id_type=MESH,
+                ).start()
+
+            return carry
+
+        lax.fori_loop(0, n_grp, step, 0)
+
+    @pl.when(me < near)
+    def _():
+        ship(send_own, got_own, 0)
+
+    for wave in range(2):
+        ship(sends.at[wave], gots.at[wave], 1 + wave)
     local = [pltpu.make_async_copy(send_own.at[me], got_own.at[me], local_sems.at[0])]
     for wave in range(2):
         local.append(

time: 25.9 us -> 24.2 us (0.934)
  Pallas kernels: 25.8 us -> 24.1 us
    pallas_call x1, Pallas kernels: 22.7 us -> 21 us  [on_device(): pl.pallas_call(functools.partial(exchange_kernel, n_grp, n_rep), out_shap...]
where the time goes in v7:
time: 24.2 us; the launch traced here: 24.1 us
  Pallas kernels  24.1 us (100%)
    pallas_call x1, Pallas kernels, on_device(): pl.pallas_call(functools.partial(exchange_kernel, n_grp, n_rep), out_shap...  21 us
    pallas_call x1, Pallas kernels, on_device(): pl.pallas_call(correlate_kernel, out_shape=jax.ShapeDtypeStruct((1, PMAX,...  3.1 us

profile of v7, /device:TPU:1, one launch (start us, length us, event | category | flops | bytes accessed | tf_op | source)
XLA Modules:
  0.0 24.1 jit_solution(5521207769876164912)
XLA Ops:
  0.0 21.0 %exchange.1 = (bf16[20,256,256]{2,1,0:T(8,128)(2,1)S(1)}, bf16[2,160,256]{2,1,0:T(8,128)(2,1)S(1)}, bf16[4,40,40,256]{3,2,1,0:T(8,128)(2,1)S(1)}) custom-call(bf16[6,10240]{1,0:T(8,128)(2,1)} %bitcast.4, s32[8,256]{1,0:T(8,128)} %bitcast.5, s32[1,160]{1,0:T(1,128)} %bitcast.6, f32[1,64]{1,0:T(1,128)} %bitcast.7), custom_call_target="tpu_custom_call" | custom-call | tf_op jit(solution)/shard_map/exchange/pallas_call | solution.py:386
  21.0 3.1 %correlate.1 = bf16[1,8,40,40,256]{4,3,2,1,0:T(8,128)(2,1)} custom-call(bf16[20,256,256]{2,1,0:T(8,128)(2,1)S(1)} %get-tuple-element.8.w_ref, bf16[2,160,256]{2,1,0:T(8,128)(2,1)S(1)} %get-tuple-element.9.ab_ref, bf16[4,40,40,256]{3,2,1,0:T(8,128)(2,1)S(1)} %get-tuple-element.10.first_ref), custom_call_target="tpu_custom_call" | custom-call | tf_op jit(solution)/shard_map/correlate/pallas_call | solution.py:419

commit v8 on v7

--- a/solution.py
+++ b/solution.py
@@ -232,7 +232,7 @@
 
             return carry
 
-        lax.fori_loop(0, n_grp, step, 0)
+        lax.fori_loop(0, n_grp, step, 0, unroll=8)
 
     @pl.when(me < near)
     def _():

time: 24.2 us -> 24.4 us (level)
  no operation moved by 1% of the time
where the time goes in v8:
time: 24.4 us; the launch traced here: 24.3 us
  Pallas kernels  24.3 us (100%)
    pallas_call x1, Pallas kernels, on_device(): pl.pallas_call(functools.partial(exchange_kernel, n_grp, n_rep), out_shap...  21.2 us
    pallas_call x1, Pallas kernels, on_device(): pl.pallas_call(correlate_kernel, out_shape=jax.ShapeDtypeStruct((1, PMAX,...  3.1 us

profile of v8, /device:TPU:1, one launch (start us, length us, event | category | flops | bytes accessed | tf_op | source)
XLA Modules:
  0.0 24.3 jit_solution(4587045844723176431)
XLA Ops:
  0.0 21.2 %exchange.1 = (bf16[20,256,256]{2,1,0:T(8,128)(2,1)S(1)}, bf16[2,160,256]{2,1,0:T(8,128)(2,1)S(1)}, bf16[4,40,40,256]{3,2,1,0:T(8,128)(2,1)S(1)}) custom-call(bf16[6,10240]{1,0:T(8,128)(2,1)} %bitcast.4, s32[8,256]{1,0:T(8,128)} %bitcast.5, s32[1,160]{1,0:T(1,128)} %bitcast.6, f32[1,64]{1,0:T(1,128)} %bitcast.7), custom_call_target="tpu_custom_call" | custom-call | tf_op jit(solution)/shard_map/exchange/pallas_call | solution.py:386
  21.2 3.1 %correlate.1 = bf16[1,8,40,40,256]{4,3,2,1,0:T(8,128)(2,1)} custom-call(bf16[20,256,256]{2,1,0:T(8,128)(2,1)S(1)} %get-tuple-element.8.w_ref, bf16[2,160,256]{2,1,0:T(8,128)(2,1)S(1)} %get-tuple-element.9.ab_ref, bf16[4,40,40,256]{3,2,1,0:T(8,128)(2,1)S(1)} %get-tuple-element.10.first_ref), custom_call_target="tpu_custom_call" | custom-call | tf_op jit(solution)/shard_map/correlate/pallas_call | solution.py:419
